TPU v7x, 256 devices: a whole 4x4x8 slice. The times are simulated.
256 devices in a mesh: tracer: 16 (over z_lo, x, core), space: 16 (over z_hi, y).
Axes of the slice: x: 4, y: 4, z: 8 (z_hi: 4, z_lo: 2; z = z_hi * 2 + z_lo), core: 2. Of those that a mesh axis runs over, the one named last changes fastest.
Arguments:
- tracers: float32 [512, 16, 288, 128], P('tracer', None, 'space'), may hold values from -6 to 6
- met_codes: bfloat16 [16, 3, 288, 128], P('tracer', None, 'space'), may hold values from -1 to 1
- met_scales: bfloat16 [16, 3, 288], P('tracer', None, 'space'), may hold values from 0.29882812 to 0.8984375
- owner_slot: int32 [16], replicated, may hold values from 0 to 15, each once
- conv_weight: float32 [288, 128], P('space'), may hold values from 0.2 to 0.9
- cloud_top: int32 [288, 128], P('space'), may hold values from 1 to 16
- emission: float32 [288, 128], P('space'), may hold values from 0.5 to 2
- region_tag: int32 [288, 128], P('space'), may hold values from 0 to 511
Outputs:
- tracers_out: float32 [512, 16, 288, 128], P('tracer', None, 'space')
Inputs may be any that keep to these rules, and one draw needn't show every extreme that they name: owner_slot names every slot 0 to 15 once.
All inputs are finite; a program needn't handle non-finite values.
Results may differ from a plain program's by a relative error of at most 0.0003.
Values may be sent and summed in bfloat16 or wider, within the bound.
A program may use at most 128 MiB of HBM per device.

v0:
```python
import jax
import jax.numpy as jnp
from jax import lax
from jax.sharding import PartitionSpec as P

SUBSTEPS = 2


def shifted(x, axis, by):
    size = lax.axis_size(axis)
    return lax.ppermute(x, axis, [(i, (i + by) % size) for i in range(size)])


def extended_2(cells, sides, width):
    for axis, dim in sides:
        count = lax.axis_size(axis)
        head = lax.slice_in_dim(cells, 0, width, axis=dim)
        tail = lax.slice_in_dim(cells, cells.shape[dim] - width, cells.shape[dim], axis=dim)
        cells = jnp.concatenate(
            [
                lax.ppermute(tail, axis, [(i, (i + 1) % count) for i in range(count)]),
                cells,
                lax.ppermute(head, axis, [((i + 1) % count, i) for i in range(count)]),
            ],
            axis=dim,
        )
    return cells


def fromm_flux(courant, left_val, left_slope, right_val, right_slope):
    upwind_left = courant * (left_val + 0.5 * (1.0 - courant) * left_slope)
    upwind_right = courant * (right_val - 0.5 * (1.0 + courant) * right_slope)
    return jnp.where(courant > 0, upwind_left, upwind_right)


def sweep_east(extended, face_courant):
    cells = extended.shape[-2] - 4
    slope = 0.5 * (extended[..., 2:, :] - extended[..., :-2, :])
    flux = fromm_flux(
        face_courant,
        extended[..., 1 : cells + 2, :],
        slope[..., 0 : cells + 1, :],
        extended[..., 2 : cells + 3, :],
        slope[..., 1 : cells + 2, :],
    )
    return extended[..., 2 : cells + 2, :] - (flux[..., 1:, :] - flux[..., :-1, :])


def sweep_north(mixing, courant_south):
    rows = mixing.shape[-1]
    widths = [(0, 0)] * (mixing.ndim - 1) + [(2, 2)]
    padded = jnp.pad(mixing, widths)
    slope = 0.5 * (padded[..., 2:] - padded[..., :-2])
    walled = courant_south * (jnp.arange(rows) > 0).astype(jnp.float32)
    flux = fromm_flux(
        walled,
        padded[..., 1 : rows + 1],
        slope[..., 0:rows],
        padded[..., 2 : rows + 2],
        slope[..., 1 : rows + 1],
    )
    upper = jnp.concatenate([flux[..., 1:], jnp.zeros_like(flux[..., :1])], axis=-1)
    return mixing - (upper - flux)


def convect(mixing, air_mass, strength, top_level):
    levels = air_mass.shape[0]
    in_cloud = (jnp.arange(levels, dtype=jnp.int32)[:, None, None] < top_level[None]).astype(
        jnp.float32
    )
    weighted = in_cloud * air_mass
    cloud_mass = jnp.sum(weighted, axis=0)
    cloud_mean = jnp.sum(weighted * mixing, axis=-3) / cloud_mass
    return mixing + strength * in_cloud * (cloud_mean[:, None] - mixing)


def later_sweeps(mixing, column_met, levels):
    mixing = sweep_north(mixing, column_met[levels : 2 * levels])
    air_mass = 1.0 + 0.5 * column_met[2 * levels : 3 * levels]
    top_level = column_met[3 * levels + 1].astype(jnp.int32)
    return convect(mixing, air_mass, column_met[3 * levels], top_level)


def local(tracers, met_codes, met_scales, owner_slot, conv_weight, cloud_top, emission, region_tag):
    tracer_count, levels, longitudes, latitudes = tracers.shape
    piece_rows = met_codes.shape[1]
    pieces = owner_slot.shape[0]
    all_values, all_scales = (
        lax.all_gather(met_codes, "tracer", axis=0, tiled=True),
        lax.all_gather(met_scales, "tracer", axis=0, tiled=True),
    )
    ordered = (
        all_values[owner_slot].astype(jnp.float32)
        * all_scales[owner_slot].astype(jnp.float32)[..., None]
    )
    met_stack = ordered.reshape(pieces * piece_rows, longitudes, latitudes)
    column_met = jnp.concatenate(
        [met_stack, conv_weight[None], cloud_top[None].astype(jnp.float32)], axis=0
    )
    first_tracer = lax.axis_index("tracer") * tracer_count
    tracer_ids = first_tracer + jnp.arange(tracer_count, dtype=jnp.int32)
    emitted = (region_tag[None] == tracer_ids[:, None, None]).astype(jnp.float32) * emission[None]
    mixing = tracers.at[:, 0].add(emitted)
    west_courant = shifted(met_stack[:levels, longitudes - 1 :, :], "space", 1)
    east_courant = jnp.concatenate([west_courant, met_stack[:levels]], axis=1)
    for substep in range(SUBSTEPS):
        extended = extended_2(mixing, (("space", 2),), 2)
        mixing = sweep_east(extended, east_courant)
        mixing = later_sweeps(mixing, column_met, levels)
    return mixing


def solution(mesh):
    placed = (
        P("tracer", None, "space", None),
        P("tracer", None, "space", None),
        P("tracer", None, "space"),
        P(),
        P("space", None),
        P("space", None),
        P("space", None),
        P("space", None),
    )
    return jax.shard_map(
        local,
        mesh=mesh,
        in_specs=placed,
        out_specs=P("tracer", None, "space", None),
        check_vma=False,
    )
```

profile of v0, /device:TPU:90, one launch (start us, length us, event | category | flops | bytes accessed | tf_op | source)
XLA Modules:
  0.0 173.0 jit_solution(1786064542822178739)
XLA Ops:
  0.0 0.0 copy-start.16
  0.0 0.0 copy-start.17
  0.0 4.9 %copy.31 = f32[32,16,18,128]{3,1,2,0:T(8,128)} copy(f32[32,16,18,128]{3,1,2,0:T(8,128)} %param.10) | data formatting | bytes 9437184
  4.9 0.0 copy-done.20
  5.0 0.0 copy-done.19
  5.0 17.3 %all_gather.7 = bf16[16,3,18]{2,1,0:T(4,128)(2,1)S(1)} all-gather(bf16[1,3,18]{2,1,0:T(4,128)(2,1)S(1)} %copy-done.19), channel_id=1, replica_groups=mesh['tracer'=16,'space'=16] {'tracer'}, dimensions={0}, use_global_device_ids=true | all-gather | bytes 1836 | tf_op jit(solution)/shard_map/all_gather | solution.py:90
  22.2 0.6 gather_fusion.1
  22.8 0.1 copy.26
  22.9 0.0 copy-done.14
  22.9 20.0 %all_gather.6 = bf16[16,3,18,128]{3,2,1,0:T(8,128)(2,1)S(1)} all-gather(bf16[1,3,18,128]{3,2,1,0:T(8,128)(2,1)S(1)} %copy-done.14), channel_id=1, replica_groups=mesh['tracer'=16,'space'=16] {'tracer'}, dimensions={0}, use_global_device_ids=true | all-gather | bytes 235008 | tf_op jit(solution)/shard_map/all_gather | solution.py:89
  42.9 0.6 gather_fusion
  43.5 0.1 bitcast_convert_fusion
  43.6 0.2 copy_multiply_fusion
  43.8 3.3 %collective-permute-start = (f32[16,1,128]{2,0,1:T(8,128)S(1)}, f32[16,1,128]{2,0,1:T(8,128)S(1)}, u32[]{:S(2)}, u32[]{:S(2)}) collective-permute-start(f32[16,1,128]{2,0,1:T(8,128)S(1)} %slice.176), channel_id=1, source_target_pairs={{0,1},{1,2},{2,3},{3,4},{4,5},{5,6},{6,7},{7,8},{8,9},{9,10},{10,1... | collective-permute-start | bytes 24584 | tf_op jit(solution)/shard_map/ppermute | solution.py:11
  47.1 0.0 copy-done.16
  47.1 0.0 copy-done.17
  47.1 2.0 %fusion.34 = f32[32,1,18,128]{3,1,2,0:T(1,128)S(1)} fusion(f32[32,16,18,128]{3,1,2,0:T(8,128)} %copy.31, f32[18,128]{1,0:T(8,128)S(1)} %copy-done.16, s32[18,128]{1,0:T(8,128)S(1)} %copy-done.17, s32[32]{0:T(128)S(1)} %iota_add_fusion), kind=kLoop, calls=%fused_computation.72 | loop fusion | flops 221184 | bytes 608384 | tf_op jit(solution)/shard_map/add | solution.py:103
  49.1 8.2 %scatter-add.4 = f32[32,16,18,128]{3,1,2,0:T(8,128)} dynamic-update-slice(f32[32,16,18,128]{3,1,2,0:T(8,128)} %copy.31, f32[32,1,18,128]{3,1,2,0:T(1,128)S(1)} %fusion.34, s32[]{:T(128)} %constant.52.clone.1, s32[]{:T(128)} %constant.52.clone.1, s32[]{:T(128)} %constant.52.clone.1, s32[]{:T(128)} %constant.52.clone.1) | dynamic-update-slice | bytes 589828 | tf_op jit(solution)/shard_map/scatter-add | solution.py:103
  57.3 1.3 fusion.41
  58.6 1.7 collective-permute-start.1
  60.3 0.4 collective-permute-start.2
  60.7 0.0 copy-done.15
  60.7 0.0 copy-done.18
  60.7 0.8 fusion.38
  61.5 0.7 subtract_multiply_fusion.1
  62.2 0.0 collective-permute-done
  62.2 0.0 slice-start
  62.3 0.0 copy-start.1
  62.3 0.0 copy-start.3
  62.3 0.0 copy-start.5
  62.3 0.0 slice-start.1
  62.3 18.6 %collective-permute-done.1 = f32[32,16,2,128]{3,1,2,0:T(8,128)S(1)} collective-permute-done((f32[32,16,2,128]{3,1,2,0:T(8,128)S(1)}, f32[32,16,2,128]{3,1,2,0:T(8,128)S(1)}, u32[]{:S(2)}, u32[]{:S(2)}) %collective-permute-start.1) | collective-permute-done | bytes 524320 | tf_op jit(solution)/shard_map/ppermute | solution.py:21
  81.0 8.4 %collective-permute-done.2 = f32[32,16,2,128]{3,1,2,0:T(8,128)S(1)} collective-permute-done((f32[32,16,2,128]{3,1,2,0:T(8,128)S(1)}, f32[32,16,2,128]{3,1,2,0:T(8,128)S(1)}, u32[]{:S(2)}, u32[]{:S(2)}) %collective-permute-start.2) | collective-permute-done | bytes 524320 | tf_op jit(solution)/shard_map/ppermute | solution.py:23
  89.3 4.5 %fusion.7 = f32[32,16,20,128]{3,1,2,0:T(8,128)S(1)} fusion(f32[32,16,2,128]{3,1,2,0:T(8,128)S(1)} %collective-permute-done.2, f32[32,16,2,128]{3,1,2,0:T(8,128)S(1)} %collective-permute-done.1, f32[32,16,18,128]{3,1,2,0:T(8,128)} %scatter-add.4), kind=kLoop, calls=%fused_computation.23 | loop fusion | flops 5242880 | bytes 11010048 | tf_op jit(solution)/shard_map/mul | solution.py:38
  93.9 0.0 copy-done.1
  93.9 0.0 copy-done.3
  93.9 0.0 copy-done.5
  93.9 0.0 slice-done
  93.9 0.0 slice-done.1
  93.9 2.4 %fusion.18 = f32[32,16,19,128]{3,1,2,0:T(8,128)S(1)} fusion(f32[32,16,18,128]{3,1,2,0:T(8,128)S(1)} %bitcast.4, f32[32,16,2,128]{3,1,2,0:T(8,128)S(1)} %collective-permute-done.2, f32[32,16,2,128]{3,1,2,0:T(8,128)S(1)} %collective-permute-done.1, f32[32,16,20,128]{3,1,2,0:T(8,128)S(1)} %fusion.7, f32[16,19,128]{2,0,1:T(8,128)S(1)} %get-tuple-element.28, ...), kind=kLoop, calls=%fused_computation.38 | loop fusion | flops 11206656 | bytes 21215232 | tf_op jit(solution)/shard_map/jit(_where)/select_n | solution.py:33
  96.4 1.0 fusion.33
  97.4 6.2 %fusion.1 = f32[32,16,18,130]{3,1,2,0:T(8,128)} fusion(f32[32,16,18,128]{3,1,2,0:T(8,128)S(1)} %fusion.33), kind=kLoop, calls=%fused_computation.9 | loop fusion | flops 2396160 | bytes 9510912 | tf_op jit(solution)/shard_map/mul | solution.py:53
  103.6 0.0 copy-done.7
  103.6 6.6 %fusion.24 = f32[32,16,18,128]{3,1,2,0:T(8,128)S(1)} fusion(f32[32,16,18,128]{3,1,2,0:T(8,128)S(1)} %fusion.33, f32[32,16,18,130]{3,1,2,0:T(8,128)} %fusion.1, f32[16,18,128]{2,0,1:T(8,128)S(1)} %copy-done.9, f32[16,18,128]{2,0,1:T(8,128)S(1)} %get-tuple-element.29, f32[16,18,128]{2,0,1:T(8,128)S(1)} %get-tuple-element.20, ...), kind=kLoop, calls=%fused_computation.48 | loop fusion | flops 8257536 | bytes 19353600 | tf_op jit(solution)/shard_map/jit(_where)/select_n | solution.py:33
  110.2 0.0 copy-start.12
  110.2 1.3 slice.191
  111.5 2.4 %multiply_reduce_fusion.1 = f32[32,18,128]{2,1,0:T(8,128)S(1)} fusion(f32[16,18,128]{2,0,1:T(8,128)S(1)} %copy-done.12, f32[32,16,18,128]{3,1,2,0:T(8,128)S(1)} %fusion.33, f32[32,16,18,128]{3,1,2,0:T(8,128)S(1)} %fusion.24, f32[32,16,18,127]{3,1,2,0:T(8,128)S(1)} %slice.191), kind=kLoop, calls=%fused_computation.68 | loop fusion | flops 4644864 | bytes 14561280 | tf_op jit(solution)/shard_map/reduce_sum | solution.py:73
  113.9 0.8 broadcast_divide_fusion.1
  114.7 4.1 %multiply_add_fusion.1 = f32[32,16,18,128]{3,1,2,0:T(8,128)S(1)} fusion(f32[32,18,128]{2,1,0:T(8,128)} %broadcast_divide_fusion.1, f32[16,18,128]{2,0,1:T(8,128)S(1)} %copy-done.11, f32[32,16,18,128]{3,1,2,0:T(8,128)S(1)} %fusion.33, f32[32,16,18,128]{3,1,2,0:T(8,128)S(1)} %fusion.24, f32[32,16,18,127]{3,1,2,0:T(8,128)} %copy-done), kind=kLoop, calls=%fused_computation.67 | loop fusion | flops 5898240 | bytes 19279872 | tf_op jit(solution)/shard_map/add | solution.py:74
  118.8 0.1 fusion.40
  118.9 0.3 collective-permute-start.3
  119.2 2.0 %collective-permute-start.4 = (f32[32,16,2,128]{3,1,2,0:T(8,128)S(1)}, f32[32,16,2,128]{3,1,2,0:T(8,128)S(1)}, u32[]{:S(2)}, u32[]{:S(2)}) collective-permute-start(f32[32,16,2,128]{3,1,2,0:T(8,128)S(1)} %get-tuple-element.22), channel_id=1, source_target_pairs={{1,0},{2,1},{3,2},{4,3},{5,4},{6,5},{7,6},{8,7},{9,8},{10,9},{11,1... | collective-permute-start | bytes 1572872 | tf_op jit(solution)/shard_map/ppermute | solution.py:23
  121.2 18.3 %collective-permute-done.3 = f32[32,16,2,128]{3,1,2,0:T(8,128)S(1)} collective-permute-done((f32[32,16,2,128]{3,1,2,0:T(8,128)S(1)}, f32[32,16,2,128]{3,1,2,0:T(8,128)S(1)}, u32[]{:S(2)}, u32[]{:S(2)}) %collective-permute-start.3) | collective-permute-done | bytes 524320 | tf_op jit(solution)/shard_map/ppermute | solution.py:21
  139.5 8.5 %collective-permute-done.4 = f32[32,16,2,128]{3,1,2,0:T(8,128)S(1)} collective-permute-done((f32[32,16,2,128]{3,1,2,0:T(8,128)S(1)}, f32[32,16,2,128]{3,1,2,0:T(8,128)S(1)}, u32[]{:S(2)}, u32[]{:S(2)}) %collective-permute-start.4) | collective-permute-done | bytes 524320 | tf_op jit(solution)/shard_map/ppermute | solution.py:23
  148.0 0.7 fusion.5
  148.7 2.4 %fusion.11 = f32[32,16,19,128]{3,1,2,0:T(8,128)S(1)} fusion(f32[32,16,18,128]{3,1,2,0:T(8,128)S(1)} %multiply_add_fusion.1, f32[32,16,2,128]{3,1,2,0:T(8,128)S(1)} %collective-permute-done.4, f32[32,16,2,128]{3,1,2,0:T(8,128)S(1)} %collective-permute-done.3, f32[32,16,20,128]{3,1,2,0:T(8,128)S(1)} %fusion.5, f32[16,19,128]{2,0,1:T(8,128)S(1)} %copy-done.6, ...), kind=kLoop, calls=%fused_computation.31 | loop fusion | flops 11206656 | bytes 21215232 | tf_op jit(solution)/shard_map/jit(_where)/select_n | solution.py:33
  151.1 0.7 fusion.30
  151.9 0.0 copy-start.8
  151.9 0.0 copy-start.10
  151.9 6.2 %fusion.3 = f32[32,16,18,130]{3,1,2,0:T(8,128)} fusion(f32[32,16,18,128]{3,1,2,0:T(8,128)S(1)} %fusion.30), kind=kLoop, calls=%fused_computation.11 | loop fusion | flops 2396160 | bytes 9510912 | tf_op jit(solution)/shard_map/mul | solution.py:53
  158.1 6.6 %fusion.27 = f32[32,16,18,128]{3,1,2,0:T(8,128)S(1)} fusion(f32[32,16,18,128]{3,1,2,0:T(8,128)S(1)} %fusion.30, f32[32,16,18,130]{3,1,2,0:T(8,128)} %fusion.3, f32[16,18,128]{2,0,1:T(8,128)S(1)} %copy-done.10, f32[16,18,128]{2,0,1:T(8,128)S(1)} %copy-done.8, f32[16,18,128]{2,0,1:T(8,128)S(1)} %get-tuple-element.20, pred[16,18,128]{2,0,1:T(8,128)(4,1)S(1)} %get-tuple-element.19), kind=kLoop, calls=%fused_computation.51 | loop fusion | flops 8257536 | bytes 19353600 | tf_op jit(solution)/shard_map/jit(_where)/select_n | solution.py:33
  164.7 1.3 slice.205
  166.0 2.3 %multiply_reduce_fusion = f32[32,18,128]{2,1,0:T(8,128)S(1)} fusion(f32[16,18,128]{2,0,1:T(8,128)S(1)} %copy-done.13, f32[32,16,18,128]{3,1,2,0:T(8,128)S(1)} %fusion.30, f32[32,16,18,128]{3,1,2,0:T(8,128)S(1)} %fusion.27, f32[32,16,18,127]{3,1,2,0:T(8,128)S(1)} %slice.205), kind=kLoop, calls=%fused_computation.65 | loop fusion | flops 4644864 | bytes 14561280 | tf_op jit(solution)/shard_map/reduce_sum | solution.py:73
  168.3 4.7 %multiply_add_fusion = f32[32,16,18,128]{3,1,2,0:T(8,128)} fusion(f32[32,18,128]{2,1,0:T(8,128)S(1)} %broadcast_divide_fusion, f32[16,18,128]{2,0,1:T(8,128)} %get-tuple-element.31, f32[32,16,18,128]{3,1,2,0:T(8,128)S(1)} %fusion.30, f32[32,16,18,128]{3,1,2,0:T(8,128)S(1)} %fusion.27, f32[32,16,18,127]{3,1,2,0:T(8,128)S(1)} %slice.205), kind=kLoop, calls=%fused_computation.64 | loop fusion | flops 5898240 | bytes 19279872 | tf_op jit(solution)/shard_map/add | solution.py:74
  (35 shorter events, 0.2 us)
Async XLA Ops:
  0.0 22.9 %copy-start.14 = (bf16[1,3,18,128]{3,2,1,0:T(8,128)(2,1)S(1)}, bf16[1,3,18,128]{3,2,1,0:T(8,128)(2,1)}, u32[]{:S(2)}) copy-start(bf16[1,3,18,128]{3,2,1,0:T(8,128)(2,1)} %param.11) | copy-start | bytes 41476
  0.0 5.0 %copy-start.19 = (bf16[1,3,18]{2,1,0:T(4,128)(2,1)S(1)}, bf16[1,3,18]{2,1,0:T(4,128)(2,1)}, u32[]{:S(2)}) copy-start(bf16[1,3,18]{2,1,0:T(4,128)(2,1)} %param.12) | copy-start | bytes 328
  0.0 4.9 %copy-start.20 = (s32[16]{0:T(128)S(1)}, s32[16]{0:T(128)}, u32[]{:S(2)}) copy-start(s32[16]{0:T(128)} %param.13) | copy-start | bytes 196
  0.0 47.1 %copy-start.16 = (f32[18,128]{1,0:T(8,128)S(1)}, f32[18,128]{1,0:T(8,128)}, u32[]{:S(2)}) copy-start(f32[18,128]{1,0:T(8,128)} %param.16) | copy-start | bytes 27652
  0.0 47.1 %copy-start.17 = (s32[18,128]{1,0:T(8,128)S(1)}, s32[18,128]{1,0:T(8,128)}, u32[]{:S(2)}) copy-start(s32[18,128]{1,0:T(8,128)} %param.17) | copy-start | bytes 27652
  4.9 55.8 %copy-start.15 = (s32[18,128]{1,0:T(8,128)S(1)}, s32[18,128]{1,0:T(8,128)}, u32[]{:S(2)}) copy-start(s32[18,128]{1,0:T(8,128)} %param.15) | copy-start | bytes 27652
  4.9 55.8 %copy-start.18 = (f32[18,128]{1,0:T(8,128)S(1)}, f32[18,128]{1,0:T(8,128)}, u32[]{:S(2)}) copy-start(f32[18,128]{1,0:T(8,128)} %param.14) | copy-start | bytes 27652
  43.8 18.4 %collective-permute-start = (f32[16,1,128]{2,0,1:T(8,128)S(1)}, f32[16,1,128]{2,0,1:T(8,128)S(1)}, u32[]{:S(2)}, u32[]{:S(2)}) collective-permute-start(f32[16,1,128]{2,0,1:T(8,128)S(1)} %slice.176), channel_id=1, source_target_pairs={{0,1},{1,2},{2,3},{3,4},{4,5},{5,6},{6,7},{7,8},{8,9},{9,10},{10,1... | collective-permute-start | bytes 24584 | tf_op jit(solution)/shard_map/ppermute | solution.py:11
  58.6 22.4 %collective-permute-start.1 = (f32[32,16,2,128]{3,1,2,0:T(8,128)S(1)}, f32[32,16,2,128]{3,1,2,0:T(8,128)S(1)}, u32[]{:S(2)}, u32[]{:S(2)}) collective-permute-start(f32[32,16,2,128]{3,1,2,0:T(8,128)S(1)} %get-tuple-element.23), channel_id=1, source_target_pairs={{0,1},{1,2},{2,3},{3,4},{4,5},{5,6},{6,7},{7,8},{8,9},{9,10},{10,1... | collective-permute-start | bytes 1572872 | tf_op jit(solution)/shard_map/ppermute | solution.py:21
  60.3 29.1 %collective-permute-start.2 = (f32[32,16,2,128]{3,1,2,0:T(8,128)S(1)}, f32[32,16,2,128]{3,1,2,0:T(8,128)S(1)}, u32[]{:S(2)}, u32[]{:S(2)}) collective-permute-start(f32[32,16,2,128]{3,1,2,0:T(8,128)S(1)} %get-tuple-element.24), channel_id=1, source_target_pairs={{1,0},{2,1},{3,2},{4,3},{5,4},{6,5},{7,6},{8,7},{9,8},{10,9},{11,1... | collective-permute-start | bytes 1572872 | tf_op jit(solution)/shard_map/ppermute | solution.py:23
  62.2 41.4 %copy-start.7 = (f32[16,18,128]{2,0,1:T(8,128)}, f32[16,18,128]{2,0,1:T(8,128)S(1)}, u32[]{:S(2)}) copy-start(f32[16,18,128]{2,0,1:T(8,128)S(1)} %get-tuple-element.29) | copy-start | bytes 442372
  62.2 31.7 %slice-start = ((s8[4718592]{0:T(1024)(128)(4,1)}), s8[4194304]{0:T(1024)(128)(4,1)S(1)}, s32[]{:S(2)}) async-start(s8[4718592]{0:T(1024)(128)(4,1)} %bitcast.3), calls=%async_computation | async-start | bytes 8388608
  62.3 31.6 %copy-start.1 = (f32[16,19,128]{2,0,1:T(8,128)}, f32[16,19,128]{2,0,1:T(8,128)S(1)}, u32[]{:S(2)}) copy-start(f32[16,19,128]{2,0,1:T(8,128)S(1)} %get-tuple-element.26) | copy-start | bytes 466948
  62.3 31.6 %copy-start.3 = (f32[16,19,128]{2,0,1:T(8,128)}, f32[16,19,128]{2,0,1:T(8,128)S(1)}, u32[]{:S(2)}) copy-start(f32[16,19,128]{2,0,1:T(8,128)S(1)} %get-tuple-element.27) | copy-start | bytes 466948
  62.3 31.6 %copy-start.5 = (f32[16,19,128]{2,0,1:T(8,128)}, f32[16,19,128]{2,0,1:T(8,128)S(1)}, u32[]{:S(2)}) copy-start(f32[16,19,128]{2,0,1:T(8,128)S(1)} %get-tuple-element.28) | copy-start | bytes 466948
  62.3 31.6 %slice-start.1 = ((s8[4718592]{0:T(1024)(128)(4,1)}), s8[524288]{0:T(1024)(128)(4,1)S(1)}, s32[]{:S(2)}) async-start(s8[4718592]{0:T(1024)(128)(4,1)} %bitcast.3), calls=%async_computation.1 | async-start | bytes 1048576
  97.4 6.2 %copy-start.9 = (f32[16,18,128]{2,0,1:T(8,128)S(1)}, f32[16,18,128]{2,0,1:T(8,128)}, u32[]{:S(2)}) copy-start(f32[16,18,128]{2,0,1:T(8,128)} %get-tuple-element.30) | copy-start | bytes 442372
  110.2 1.3 copy-start.12
  111.5 2.4 %copy-start = (f32[32,16,18,127]{3,1,2,0:T(8,128)}, f32[32,16,18,127]{3,1,2,0:T(8,128)S(1)}, u32[]{:S(2)}) copy-start(f32[32,16,18,127]{3,1,2,0:T(8,128)S(1)} %slice.191) | copy-start | bytes 14045188
  111.5 3.2 %copy-start.11 = (f32[16,18,128]{2,0,1:T(8,128)S(1)}, f32[16,18,128]{2,0,1:T(8,128)}, u32[]{:S(2)}) copy-start(f32[16,18,128]{2,0,1:T(8,128)} %get-tuple-element.31) | copy-start | bytes 442372
  118.9 20.6 %collective-permute-start.3 = (f32[32,16,2,128]{3,1,2,0:T(8,128)S(1)}, f32[32,16,2,128]{3,1,2,0:T(8,128)S(1)}, u32[]{:S(2)}, u32[]{:S(2)}) collective-permute-start(f32[32,16,2,128]{3,1,2,0:T(8,128)S(1)} %get-tuple-element.21), channel_id=1, source_target_pairs={{0,1},{1,2},{2,3},{3,4},{4,5},{5,6},{6,7},{7,8},{8,9},{9,10},{10,1... | collective-permute-start | bytes 1572872 | tf_op jit(solution)/shard_map/ppermute | solution.py:21
  119.2 29.5 %copy-start.2 = (f32[16,19,128]{2,0,1:T(8,128)S(1)}, f32[16,19,128]{2,0,1:T(8,128)}, u32[]{:S(2)}) copy-start(f32[16,19,128]{2,0,1:T(8,128)} %copy-done.1) | copy-start | bytes 466948
  119.2 29.5 %copy-start.4 = (f32[16,19,128]{2,0,1:T(8,128)S(1)}, f32[16,19,128]{2,0,1:T(8,128)}, u32[]{:S(2)}) copy-start(f32[16,19,128]{2,0,1:T(8,128)} %copy-done.3) | copy-start | bytes 466948
  119.2 29.5 %copy-start.6 = (f32[16,19,128]{2,0,1:T(8,128)S(1)}, f32[16,19,128]{2,0,1:T(8,128)}, u32[]{:S(2)}) copy-start(f32[16,19,128]{2,0,1:T(8,128)} %copy-done.5) | copy-start | bytes 466948
  119.2 28.8 %collective-permute-start.4 = (f32[32,16,2,128]{3,1,2,0:T(8,128)S(1)}, f32[32,16,2,128]{3,1,2,0:T(8,128)S(1)}, u32[]{:S(2)}, u32[]{:S(2)}) collective-permute-start(f32[32,16,2,128]{3,1,2,0:T(8,128)S(1)} %get-tuple-element.22), channel_id=1, source_target_pairs={{1,0},{2,1},{3,2},{4,3},{5,4},{6,5},{7,6},{8,7},{9,8},{10,9},{11,1... | collective-permute-start | bytes 1572872 | tf_op jit(solution)/shard_map/ppermute | solution.py:23
  151.9 6.2 %copy-start.8 = (f32[16,18,128]{2,0,1:T(8,128)S(1)}, f32[16,18,128]{2,0,1:T(8,128)}, u32[]{:S(2)}) copy-start(f32[16,18,128]{2,0,1:T(8,128)} %copy-done.7) | copy-start | bytes 442372
  151.9 6.2 %copy-start.10 = (f32[16,18,128]{2,0,1:T(8,128)S(1)}, f32[16,18,128]{2,0,1:T(8,128)}, u32[]{:S(2)}) copy-start(f32[16,18,128]{2,0,1:T(8,128)} %get-tuple-element.30) | copy-start | bytes 442372
  164.7 1.3 copy-start.13
where the time goes:
time: 173 us
  other arithmetic  55.4 us (32%)
  waiting for transfers between devices  53.8 us (31%)
  blocking collectives  37.3 us (22%)
  local copies, waits for them, and re-layouts  18.4 us (11%)
  starting transfers between devices  7.71 us (4%)
    ppermute x2, waiting for transfers between devices, extended_2(): lax.ppermute(tail, axis, [(i, (i + 1) % count) for i in range(count)])  36.9 us
    all_gather x1, blocking collectives, local(): lax.all_gather(met_codes, 'tracer', axis=0, tiled=True)  20 us
    select_n x4, other arithmetic, fromm_flux(): return jnp.where(courant > 0, upwind_left, upwind_right)  18 us
    all_gather x1, blocking collectives, local(): lax.all_gather(met_scales, 'tracer', axis=0, tiled=True)  17.3 us
    ppermute x2, waiting for transfers between devices, extended_2(): lax.ppermute(head, axis, [((i + 1) % count, i) for i in range(count)])  16.9 us
    mul x2, other arithmetic, sweep_north(): slope = 0.5 * (padded[..., 2:] - padded[..., :-2])  12.4 us
    add x2, other arithmetic, convect(): return mixing + strength * in_cloud * (cloud_mean[:, None] - mixing)  8.79 us
    scatter-add x1, local copies, waits for them, and re-layouts, local(): mixing = tracers.at[:, 0].add(emitted)  8.2 us
  transfers between devices with their start and end apart: 5, of which 4 were waited for; matrix products, arithmetic and copies ran while one was open for 8% of the time, Pallas kernels for 0%

commit v1 on v0

v1 whole, which is shorter than its diff:
```python
import functools

import jax
import jax.numpy as jnp
from jax import lax
from jax.experimental import pallas as pl
from jax.experimental.pallas import tpu as pltpu
from jax.sharding import PartitionSpec as P

MESH = pl.DeviceIdType.MESH
EAST, WEST = 0, 1
HIGH, LOW = 0, 1
UNROLL = 4
BLOCKS = 4
FIELDS = 12
ROW_PITCH = 24
PIECE_ROWS = 80


def face_parts(c):
    size = jnp.abs(c)
    bend = 0.25 * size * (1.0 - size)
    up = c > 0
    zero = jnp.zeros_like(c)
    return (
        jnp.where(up, -bend, zero),
        jnp.where(up, c, -bend),
        jnp.where(up, bend, c),
        jnp.where(up, zero, bend),
    )


def column_step(cells, parts):
    ea, eb, ec, ed, ee, na, nb, nc, nd, ne, share, cloud = parts
    x = ea * cells[0] + eb * cells[1] + ec * cells[2] + ed * cells[3] + ee * cells[4]
    lanes = x.ndim - 1
    size = x.shape[-1]
    y = (
        nc * x
        + na * pltpu.roll(x, 2, lanes)
        + nb * pltpu.roll(x, 1, lanes)
        + nd * pltpu.roll(x, size - 1, lanes)
        + ne * pltpu.roll(x, size - 2, lanes)
    )
    mean = jnp.sum(share * y, axis=-2, keepdims=True)
    return y + cloud * mean


def step_kernel(
    tracer_devices,
    space_devices,
    x_hbm,
    codes_ref,
    scales_ref,
    slot_ref,
    strength_ref,
    top_ref,
    emission_ref,
    tag_ref,
    out_hbm,
    q0,
    q1,
    pieces,
    staged,
    rows,
    met,
    coef,
    west_c,
    east_c,
    halo_out,
    halo_in,
    load_sem,
    store_sem,
    piece_send,
    piece_recv,
    west_send,
    west_recv,
    halo_send,
    halo_recv,
):
    count, lons, levels, lats = x_hbm.shape
    last = lons - 1
    t_me = lax.axis_index("tracer")
    s_me = lax.axis_index("space")
    east = {"space": lax.rem(s_me + 1, space_devices)}
    west = {"space": lax.rem(s_me + space_devices - 1, space_devices)}
    toward = (east, west)
    block = count // BLOCKS

    loads = [
        pltpu.make_async_copy(x_hbm.at[:, lo:hi], q0.at[:, lo:hi], load_sem.at[n])
        for n, (lo, hi) in enumerate(((0, 2), (lons - 2, lons), (2, lons - 2)))
    ]
    for copy in loads:
        copy.start()

    barrier = pltpu.get_barrier_semaphore()
    for k in range(1, tracer_devices):
        pl.semaphore_signal(
            barrier,
            inc=1,
            device_id={"tracer": lax.rem(t_me + k, tracer_devices)},
            device_id_type=MESH,
        )
    for to in toward:
        pl.semaphore_signal(barrier, inc=1, device_id=to, device_id_type=MESH)

    staged[...] = jnp.zeros_like(staged)
    for r in range(codes_ref.shape[1]):
        staged[r * ROW_PITCH : r * ROW_PITCH + lons, :] = codes_ref[0, r].astype(jnp.float32)
        staged[r * ROW_PITCH + lons : r * ROW_PITCH + lons + 1, 0:lons] = scales_ref[
            0, r : r + 1, :
        ].astype(jnp.float32)
    pieces[t_me] = staged[...].astype(jnp.bfloat16)

    pl.semaphore_wait(barrier, tracer_devices - 1 + 2)

    piece_copies = []
    for k in range(1, tracer_devices):
        copy = pltpu.make_async_remote_copy(
            src_ref=pieces.at[t_me],
            dst_ref=pieces.at[t_me],
            send_sem=piece_send.at[k],
            recv_sem=piece_recv.at[k],
            device_id={"tracer": lax.rem(t_me + k, tracer_devices)},
            device_id_type=MESH,
        )
        copy.start()
        piece_copies.append(copy)

    first = t_me * count
    level_row = lax.broadcasted_iota(jnp.int32, (8, lats), 0)

    def emit(lon):
        tag = jnp.where(level_row == 0, tag_ref[pl.ds(lon, 1), :], -1)
        amount = jnp.broadcast_to(emission_ref[pl.ds(lon, 1), :], (8, lats))

        def some(n, _):
            for u in range(UNROLL):
                t = n * UNROLL + u
                old = q0[t, lon, 0:8, :]
                q0[t, lon, 0:8, :] = old + jnp.where(tag == first + t, amount, 0.0)
            return 0

        lax.fori_loop(0, count // UNROLL, some, 0)

    loads[0].wait()
    loads[1].wait()
    for lon in (0, 1, last - 1, last):
        emit(lon)

    def halo_copy(substep, way, part, blk):
        picked = (substep, way, part, pl.ds(blk * block, block))
        return pltpu.make_async_remote_copy(
            src_ref=halo_out.at[picked],
            dst_ref=halo_in.at[picked],
            send_sem=halo_send.at[substep, way, part, blk],
            recv_sem=halo_recv.at[substep, way, part, blk],
            device_id=toward[way],
            device_id_type=MESH,
        )

    def each_block(act):
        def one(blk, _):
            act(blk)
            return 0

        lax.fori_loop(0, BLOCKS, one, 0)

    def stage_high(q, substep, way, blk):
        lon = last if way == EAST else 0

        def some(n, _):
            t = blk * block + n * UNROLL
            halo_out[substep, way, HIGH, pl.ds(t, UNROLL)] = q[pl.ds(t, UNROLL), lon].astype(
                jnp.bfloat16
            )
            return 0

        lax.fori_loop(0, block // UNROLL, some, 0)

    def stage_low(q, substep, way, blk):
        near, far = (last, last - 1) if way == EAST else (0, 1)
        if way == EAST:
            bend = 0.25 * (1.0 - east_c[...])
        else:
            bend = 0.25 * (1.0 + west_c[...])

        def some(n, _):
            t = pl.ds(blk * block + n * UNROLL, UNROLL)
            high = halo_out[substep, way, HIGH, t].astype(jnp.float32)
            rest = (q[t, near] - high) - bend * q[t, far]
            halo_out[substep, way, LOW, t] = rest.astype(jnp.bfloat16)
            return 0

        lax.fori_loop(0, block // UNROLL, some, 0)

    def first_highs(blk):
        for way in (EAST, WEST):
            stage_high(q0, 0, way, blk)
            halo_copy(0, way, HIGH, blk).start()

    each_block(first_highs)

    loads[2].wait()

    def emit_inside(n, _):
        emit(n + 2)
        return 0

    lax.fori_loop(0, lons - 4, emit_inside, 0)

    for copy in piece_copies:
        copy.wait_recv()

    piece_count = slot_ref.shape[0]
    for j in range(piece_count):
        held = pieces[slot_ref[j]].astype(jnp.float32)
        rows[j * 3 * ROW_PITCH : (j + 1) * 3 * ROW_PITCH, :] = held[: 3 * ROW_PITCH]
    stack = 3 * piece_count
    scales = rows[pl.ds(lons, stack, stride=ROW_PITCH), :]
    for lon in range(lons):
        code = rows[pl.ds(lon, stack, stride=ROW_PITCH), :]
        met[lon] = code * scales[:, lon : lon + 1]

    east_c[...] = met[last, 0:levels, :]
    west_copy = pltpu.make_async_remote_copy(
        src_ref=east_c,
        dst_ref=west_c,
        send_sem=west_send,
        recv_sem=west_recv,
        device_id=east,
        device_id_type=MESH,
    )
    west_copy.start()

    def first_lows(way):
        def act(blk):
            stage_low(q0, 0, way, blk)
            halo_copy(0, way, LOW, blk).start()

        each_block(act)

    first_lows(EAST)

    lane = lax.broadcasted_iota(jnp.int32, (levels, lats), 1)
    level = lax.broadcasted_iota(jnp.int32, (levels, lats), 0)

    def east_parts(lon, before, here):
        la, lb, lc, ld = face_parts(before)
        ra, rb, rc, rd = face_parts(here)
        coef[lon, 0] = la
        coef[lon, 1] = lb - ra
        coef[lon, 2] = 1.0 + lc - rb
        coef[lon, 3] = ld - rc
        coef[lon, 4] = -rd

    def other_parts(lon):
        south = jnp.where(lane > 0, met[lon, levels : 2 * levels, :], 0.0)
        sa, sb, sc, sd = face_parts(south)
        ua, ub, uc, ud = (pltpu.roll(p, lats - 1, 1) for p in (sa, sb, sc, sd))
        air = 1.0 + 0.5 * met[lon, 2 * levels : 3 * levels, :]
        cloud = (level < top_ref[pl.ds(lon, 1), :]).astype(jnp.float32)
        strength = strength_ref[pl.ds(lon, 1), :]
        weighted = cloud * air
        mass = jnp.sum(weighted, axis=0, keepdims=True)
        keep = 1.0 - strength * cloud
        coef[lon, 5] = keep * jnp.where(lane > 1, sa, 0.0)
        coef[lon, 6] = keep * jnp.where(lane > 0, sb - ua, 0.0)
        coef[lon, 7] = keep * (1.0 + sc - ub)
        coef[lon, 8] = keep * jnp.where(lane < lats - 1, sd - uc, 0.0)
        coef[lon, 9] = keep * jnp.where(lane < lats - 2, -ud, 0.0)
        coef[lon, 10] = strength * weighted / (mass * keep)
        coef[lon, 11] = cloud

    def all_parts(lon, _):
        east_parts(lon, met[lon - 1, 0:levels, :], met[lon, 0:levels, :])
        other_parts(lon)
        return 0

    lax.fori_loop(1, lons, all_parts, 0)
    other_parts(0)
    coef[last, 4] = -jnp.minimum(east_c[...], 0.0)

    def inside(source, target, start, stop):
        def one(lon, _):
            parts = tuple(coef[lon, f] for f in range(FIELDS))

            def some(n, _):
                t = pl.ds(n * UNROLL, UNROLL)
                cells = [source[t, lon + d] for d in (-2, -1, 0, 1, 2)]
                target[t, lon] = column_step(cells, parts)
                return 0

            lax.fori_loop(0, count // UNROLL, some, 0)
            return 0

        lax.fori_loop(start, stop, one, 0)

    def edges(source, target, substep, blk):
        for lon in (0, 1, last - 1, last):
            parts = tuple(coef[lon, f] for f in range(FIELDS))

            def some(n, _):
                t = pl.ds(blk * block + n * UNROLL, UNROLL)

                def cell(place):
                    if 0 <= place <= last:
                        return source[t, place]
                    way = EAST if place < 0 else WEST
                    part = HIGH if place in (-1, last + 1) else LOW
                    return halo_in[substep, way, part, t].astype(jnp.float32)

                cells = [cell(lon + d) for d in (-2, -1, 0, 1, 2)]
                target[t, lon] = column_step(cells, parts)
                return 0

            lax.fori_loop(0, block // UNROLL, some, 0)

    middle = 2 + (lons - 4) // 2
    inside(q0, q1, 2, middle)
    west_copy.wait()
    first_lows(WEST)
    east_parts(0, west_c[...], met[0, 0:levels, :])
    coef[0, 0] = jnp.maximum(west_c[...], 0.0)
    inside(q0, q1, middle, lons - 2)

    def first_edges(blk):
        for way in (EAST, WEST):
            for part in (HIGH, LOW):
                halo_copy(0, way, part, blk).wait_recv()
        edges(q0, q1, 0, blk)
        for way in (EAST, WEST):
            stage_high(q1, 1, way, blk)
            stage_low(q1, 1, way, blk)
            for part in (HIGH, LOW):
                halo_copy(1, way, part, blk).start()

    each_block(first_edges)

    inside(q1, q0, 2, lons - 2)
    inner = pltpu.make_async_copy(
        q0.at[:, 2 : lons - 2], out_hbm.at[:, 2 : lons - 2], store_sem.at[0]
    )
    inner.start()

    def second_edges(blk):
        for way in (EAST, WEST):
            for part in (HIGH, LOW):
                halo_copy(1, way, part, blk).wait_recv()
        edges(q1, q0, 1, blk)

    each_block(second_edges)
    outer = [
        pltpu.make_async_copy(q0.at[:, lo:hi], out_hbm.at[:, lo:hi], store_sem.at[n])
        for n, (lo, hi) in ((1, (0, 2)), (2, (lons - 2, lons)))
    ]
    for copy in outer:
        copy.start()

    def drain(blk):
        for substep in (0, 1):
            for way in (EAST, WEST):
                for part in (HIGH, LOW):
                    halo_copy(substep, way, part, blk).wait_send()

    each_block(drain)
    for copy in piece_copies:
        copy.wait_send()
    inner.wait()
    for copy in outer:
        copy.wait()


def local(tracer_devices, space_devices, tracers, met_codes, met_scales, owner_slot, conv_weight,
          cloud_top, emission, region_tag):
    by_lon = jnp.transpose(tracers, (0, 2, 1, 3))
    count, lons, levels, lats = by_lon.shape
    pieces = owner_slot.shape[0]
    stack = pieces * met_codes.shape[1]
    halo = (2, 2, 2, count, levels, lats)
    vmem = pl.BlockSpec(memory_space=pltpu.VMEM)
    hbm = pl.BlockSpec(memory_space=pl.ANY)
    out = pl.pallas_call(
        functools.partial(step_kernel, tracer_devices, space_devices),
        out_shape=jax.ShapeDtypeStruct(by_lon.shape, jnp.float32),
        in_specs=[hbm, vmem, vmem, pl.BlockSpec(memory_space=pltpu.SMEM)] + [vmem] * 4,
        out_specs=hbm,
        scratch_shapes=[
            pltpu.VMEM(by_lon.shape, jnp.float32),
            pltpu.VMEM(by_lon.shape, jnp.float32),
            pltpu.VMEM((pieces, PIECE_ROWS, lats), jnp.bfloat16),
            pltpu.VMEM((PIECE_ROWS, lats), jnp.float32),
            pltpu.VMEM((pieces * 3 * ROW_PITCH, lats), jnp.float32),
            pltpu.VMEM((lons, stack, lats), jnp.float32),
            pltpu.VMEM((lons, FIELDS, levels, lats), jnp.float32),
            pltpu.VMEM((levels, lats), jnp.float32),
            pltpu.VMEM((levels, lats), jnp.float32),
            pltpu.VMEM(halo, jnp.bfloat16),
            pltpu.VMEM(halo, jnp.bfloat16),
            pltpu.SemaphoreType.DMA((3,)),
            pltpu.SemaphoreType.DMA((3,)),
            pltpu.SemaphoreType.DMA((pieces,)),
            pltpu.SemaphoreType.DMA((pieces,)),
            pltpu.SemaphoreType.DMA,
            pltpu.SemaphoreType.DMA,
            pltpu.SemaphoreType.DMA((2, 2, 2, BLOCKS)),
            pltpu.SemaphoreType.DMA((2, 2, 2, BLOCKS)),
        ],
        compiler_params=pltpu.CompilerParams(
            collective_id=0, has_side_effects=True, vmem_limit_bytes=48 * 1024 * 1024
        ),
        name="transport_step",
    )(by_lon, met_codes, met_scales, owner_slot, conv_weight, cloud_top, emission, region_tag)
    return jnp.transpose(out, (0, 2, 1, 3))


def solution(mesh):
    placed = (
        P("tracer", None, "space", None),
        P("tracer", None, "space", None),
        P("tracer", None, "space"),
        P(),
        P("space", None),
        P("space", None),
        P("space", None),
        P("space", None),
    )
    return jax.shard_map(
        functools.partial(local, mesh.shape["tracer"], mesh.shape["space"]),
        mesh=mesh,
        in_specs=placed,
        out_specs=P("tracer", None, "space", None),
        check_vma=False,
    )
```

time: 173 us -> 63.6 us (0.37)
  the two profiles are of different devices: /device:TPU:90 before, /device:TPU:1 now
where the time goes in v1:
time: 63.6 us; the launch traced here: 63.2 us
  Pallas kernels  56.1 us (88%)
  local copies, waits for them, and re-layouts  7.07 us (11%)
    pallas_call x1, Pallas kernels, local(): pl.pallas_call(functools.partial(step_kernel, tracer_devices, space_devic...  56.1 us
    unnamed x15, local copies, waits for them, and re-layouts  7.07 us

profile of v1, /device:TPU:1, one launch (start us, length us, event | category | flops | bytes accessed | tf_op | source)
XLA Modules:
  0.0 63.2 jit_solution(4449827752408570211)
XLA Ops:
  0.0 0.0 copy-start
  0.0 0.7 %copy-done = bf16[1,3,18,128]{3,2,1,0:T(8,128)(2,1)S(1)} copy-done((bf16[1,3,18,128]{3,2,1,0:T(8,128)(2,1)S(1)}, bf16[1,3,18,128]{3,2,1,0:T(8,128)(2,1)}, u32[]{:S(2)}) %copy-start) | copy-done | bytes 13848
  0.7 0.0 copy-start.1
  0.7 0.7 %copy-done.1 = f32[18,128]{1,0:T(8,128)S(1)} copy-done((f32[18,128]{1,0:T(8,128)S(1)}, f32[18,128]{1,0:T(8,128)}, u32[]{:S(2)}) %copy-start.1) | copy-done | bytes 9240
  1.4 0.0 copy-start.2
  1.4 0.7 %copy-done.2 = s32[18,128]{1,0:T(8,128)S(1)} copy-done((s32[18,128]{1,0:T(8,128)S(1)}, s32[18,128]{1,0:T(8,128)}, u32[]{:S(2)}) %copy-start.2) | copy-done | bytes 9240
  2.1 0.0 copy-start.3
  2.1 0.7 %copy-done.3 = f32[18,128]{1,0:T(8,128)S(1)} copy-done((f32[18,128]{1,0:T(8,128)S(1)}, f32[18,128]{1,0:T(8,128)}, u32[]{:S(2)}) %copy-start.3) | copy-done | bytes 9240
  2.8 0.0 copy-start.4
  2.8 0.7 %copy-done.4 = s32[18,128]{1,0:T(8,128)S(1)} copy-done((s32[18,128]{1,0:T(8,128)S(1)}, s32[18,128]{1,0:T(8,128)}, u32[]{:S(2)}) %copy-start.4) | copy-done | bytes 9240
  3.6 0.0 copy-start.5
  3.6 0.7 %copy-done.5 = bf16[1,3,18]{2,1,0:T(4,128)(2,1)S(1)} copy-done((bf16[1,3,18]{2,1,0:T(4,128)(2,1)S(1)}, bf16[1,3,18]{2,1,0:T(4,128)(2,1)}, u32[]{:S(2)}) %copy-start.5) | copy-done | bytes 132
  4.2 0.0 copy-start.6
  4.2 0.7 %copy-done.6 = s32[16]{0:T(128)S(1)} copy-done((s32[16]{0:T(128)S(1)}, s32[16]{0:T(128)}, u32[]{:S(2)}) %copy-start.6) | copy-done | bytes 88
  4.9 56.1 %transport_step.1 = f32[32,18,16,128]{3,2,1,0:T(8,128)S(1)} custom-call(f32[32,18,16,128]{3,2,1,0:T(8,128)} %bitcast.3, bf16[1,3,18,128]{3,2,1,0:T(8,128)(2,1)S(1)} %copy-done, bf16[1,3,18]{2,1,0:T(4,128)(2,1)S(1)} %copy-done.5, s32[16]{0:T(128)S(1)} %copy-done.6, f32[18,128]{1,0:T(8,128)S(1)} %copy-done.1, s32[18,128]{1,0:T(8,128)S(1)} %copy-done.2, ...), custom_call_target="tpu_custom_call" | custom-call | tf_op jit(solution)/shard_map/transport_step/pallas_call | solution.py:384
  61.0 2.2 %copy.10 = f32[32,16,18,128]{3,1,2,0:T(8,128)} copy(f32[32,16,18,128]{3,1,2,0:T(8,128)S(1)} %bitcast.2) | data formatting | bytes 9437184
Async XLA Ops:
  0.0 0.7 %copy-start = (bf16[1,3,18,128]{3,2,1,0:T(8,128)(2,1)S(1)}, bf16[1,3,18,128]{3,2,1,0:T(8,128)(2,1)}, u32[]{:S(2)}) copy-start(bf16[1,3,18,128]{3,2,1,0:T(8,128)(2,1)} %codes_ref.1) | copy-start | bytes 41476
  0.7 0.7 %copy-start.1 = (f32[18,128]{1,0:T(8,128)S(1)}, f32[18,128]{1,0:T(8,128)}, u32[]{:S(2)}) copy-start(f32[18,128]{1,0:T(8,128)} %strength_ref.1) | copy-start | bytes 27652
  1.4 0.7 %copy-start.2 = (s32[18,128]{1,0:T(8,128)S(1)}, s32[18,128]{1,0:T(8,128)}, u32[]{:S(2)}) copy-start(s32[18,128]{1,0:T(8,128)} %top_ref.1) | copy-start | bytes 27652
  2.1 0.7 %copy-start.3 = (f32[18,128]{1,0:T(8,128)S(1)}, f32[18,128]{1,0:T(8,128)}, u32[]{:S(2)}) copy-start(f32[18,128]{1,0:T(8,128)} %emission_ref.1) | copy-start | bytes 27652
  2.8 0.7 %copy-start.4 = (s32[18,128]{1,0:T(8,128)S(1)}, s32[18,128]{1,0:T(8,128)}, u32[]{:S(2)}) copy-start(s32[18,128]{1,0:T(8,128)} %tag_ref.1) | copy-start | bytes 27652
  3.6 0.7 %copy-start.5 = (bf16[1,3,18]{2,1,0:T(4,128)(2,1)S(1)}, bf16[1,3,18]{2,1,0:T(4,128)(2,1)}, u32[]{:S(2)}) copy-start(bf16[1,3,18]{2,1,0:T(4,128)(2,1)} %scales_ref.1) | copy-start | bytes 328
  4.2 0.7 %copy-start.6 = (s32[16]{0:T(128)S(1)}, s32[16]{0:T(128)}, u32[]{:S(2)}) copy-start(s32[16]{0:T(128)} %slot_ref.1) | copy-start | bytes 196

commit v2 on v1

v2 whole, which is shorter than its diff:
```python
import functools

import jax
import jax.numpy as jnp
from jax import lax
from jax.experimental import pallas as pl
from jax.experimental.pallas import tpu as pltpu
from jax.sharding import PartitionSpec as P

MESH = pl.DeviceIdType.MESH
EAST, WEST = 0, 1
HIGH, LOW = 0, 1
BLOCKS = 4
FIELDS = 12
ROW_PITCH = 24
PIECE_ROWS = 80
CORES = 2
PAIR = 2


def face_parts(c):
    size = jnp.abs(c)
    bend = 0.25 * size * (1.0 - size)
    up = c > 0
    zero = jnp.zeros_like(c)
    return (
        jnp.where(up, -bend, zero),
        jnp.where(up, c, -bend),
        jnp.where(up, bend, c),
        jnp.where(up, zero, bend),
    )


def column_step(cells, parts, shift):
    ea, eb, ec, ed, ee, na, nb, nc, nd, ne, share, cloud = parts
    x = ea * cells[0] + eb * cells[1] + ec * cells[2] + ed * cells[3] + ee * cells[4]
    count, levels, lats = x.shape
    high = x.astype(jnp.bfloat16)
    low = (x - high.astype(jnp.float32)).astype(jnp.bfloat16)
    both = jnp.concatenate([high, low], axis=-1).reshape(count * levels, 2 * lats)
    moved = jnp.dot(both, shift, preferred_element_type=jnp.float32)
    moved = moved.reshape(count, levels, 2 * lats)
    y = (
        nc * x
        + nb * pltpu.roll(x, 1, 2)
        + nd * pltpu.roll(x, lats - 1, 2)
        + na * moved[..., :lats]
        + ne * moved[..., lats:]
    )
    mean = jnp.sum(share * y, axis=-2, keepdims=True)
    return y + cloud * mean


def step_kernel(
    tracer_devices,
    space_devices,
    x_hbm,
    codes_hbm,
    scales_hbm,
    slot_hbm,
    strength_hbm,
    top_hbm,
    emission_hbm,
    tag_hbm,
    out_ref,
    q0,
    q1,
    codes_ref,
    scales_ref,
    slot_ref,
    strength_ref,
    top_ref,
    emission_ref,
    tag_ref,
    pieces,
    staged,
    rows,
    met,
    coef,
    edge_coef,
    shift_ref,
    west_c,
    east_c,
    far_out,
    near_in,
    far_in,
    halo_out,
    halo_in,
    load_sem,
    piece_send,
    piece_recv,
    pass_send,
    pass_recv,
    west_send,
    west_recv,
    raw_send,
    raw_recv,
    halo_send,
    halo_recv,
):
    count, lons, levels, lats = x_hbm.shape
    last = lons - 1
    t_me = lax.axis_index("tracer")
    s_me = lax.axis_index("space")
    east = {"space": lax.rem(s_me + 1, space_devices)}
    west = {"space": lax.rem(s_me + space_devices - 1, space_devices)}
    toward = (east, west)
    sibling = {"tracer": t_me + 1 - 2 * lax.rem(t_me, CORES)}
    chips = tracer_devices // CORES
    block = count // BLOCKS

    def peer(k):
        return lax.rem(t_me + CORES * k, tracer_devices)

    small = (
        (codes_hbm, codes_ref),
        (scales_hbm, scales_ref),
        (tag_hbm, tag_ref),
        (emission_hbm, emission_ref),
        (slot_hbm, slot_ref),
        (strength_hbm, strength_ref),
        (top_hbm, top_ref),
    )
    loads = [
        pltpu.make_async_copy(src, dst, load_sem.at[n]) for n, (src, dst) in enumerate(small)
    ]
    cells = [
        pltpu.make_async_copy(x_hbm.at[:, lo:hi], q0.at[:, lo:hi], load_sem.at[len(small) + n])
        for n, (lo, hi) in enumerate(((0, 2), (lons - 2, lons), (2, lons - 2)))
    ]
    for copy in loads + cells:
        copy.start()

    barrier = pltpu.get_barrier_semaphore()
    for k in range(1, chips):
        pl.semaphore_signal(barrier, inc=1, device_id={"tracer": peer(k)}, device_id_type=MESH)
    for to in (sibling, east, west):
        pl.semaphore_signal(barrier, inc=1, device_id=to, device_id_type=MESH)

    staged[...] = jnp.zeros_like(staged)
    loads[0].wait()
    loads[1].wait()
    for r in range(codes_ref.shape[1]):
        staged[r * ROW_PITCH : r * ROW_PITCH + lons, :] = codes_ref[0, r].astype(jnp.float32)
        staged[r * ROW_PITCH + lons : r * ROW_PITCH + lons + 1, 0:lons] = scales_ref[
            0, r : r + 1, :
        ].astype(jnp.float32)
    pieces[t_me] = staged[...].astype(jnp.bfloat16)

    pl.semaphore_wait(barrier, chips - 1 + 3)

    def pass_on(k):
        held = pieces.at[peer(chips - k)]
        return pltpu.make_async_remote_copy(
            src_ref=held,
            dst_ref=held,
            send_sem=pass_send.at[k],
            recv_sem=pass_recv.at[k],
            device_id=sibling,
            device_id_type=MESH,
        )

    piece_copies = []
    for k in range(1, chips):
        copy = pltpu.make_async_remote_copy(
            src_ref=pieces.at[t_me],
            dst_ref=pieces.at[t_me],
            send_sem=piece_send.at[k],
            recv_sem=piece_recv.at[k],
            device_id={"tracer": peer(k)},
            device_id_type=MESH,
        )
        copy.start()
        piece_copies.append(copy)
    pass_on(0).start()

    for copy in loads[2:]:
        copy.wait()
    ids = t_me * count + lax.broadcasted_iota(jnp.int32, (count, 8, lats), 0)
    level_row = lax.broadcasted_iota(jnp.int32, (8, lats), 0)

    def emit(lon):
        tag = jnp.where(level_row == 0, tag_ref[pl.ds(lon, 1), :], -1)
        amount = jnp.broadcast_to(emission_ref[pl.ds(lon, 1), :], (8, lats))
        q0[:, lon, 0:8, :] += jnp.where(tag[None] == ids, amount[None], 0.0)

    def each_block(act):
        def one(blk, _):
            act(blk)
            return 0

        lax.fori_loop(0, BLOCKS, one, 0)

    def raw_copies(way, blk):
        part = pl.ds(blk * block, block)
        near = q0.at[part, last if way == EAST else 0]
        pairs = ((near, near_in.at[way, part]), (far_out.at[way, part], far_in.at[way, part]))
        return [
            pltpu.make_async_remote_copy(
                src_ref=src,
                dst_ref=dst,
                send_sem=raw_send.at[n, way, blk],
                recv_sem=raw_recv.at[n, way, blk],
                device_id=toward[way],
                device_id_type=MESH,
            )
            for n, (src, dst) in enumerate(pairs)
        ]

    cells[0].wait()
    cells[1].wait()
    for lon in (0, 1, last - 1, last):
        emit(lon)
    far_out[EAST] = q0[:, last - 1].astype(jnp.bfloat16)
    far_out[WEST] = q0[:, 1].astype(jnp.bfloat16)

    def first_sends(blk):
        for way in (EAST, WEST):
            for copy in raw_copies(way, blk):
                copy.start()

    each_block(first_sends)

    for k, copy in enumerate(piece_copies, 1):
        copy.wait_recv()
        pass_on(k).start()

    cells[2].wait()

    def emit_inside(n, _):
        emit(n + 2)
        return 0

    lax.fori_loop(0, lons - 4, emit_inside, 0)

    source = lax.broadcasted_iota(jnp.int32, (2 * lats, 2 * lats), 0) % lats
    target = lax.broadcasted_iota(jnp.int32, (2 * lats, 2 * lats), 1)
    wanted = jnp.where(target < lats, target - 2, target - lats + 2)
    shift_ref[...] = jnp.where(source == wanted, 1.0, 0.0).astype(jnp.bfloat16)

    for k in range(chips):
        pass_on(k).wait_recv()

    piece_count = slot_ref.shape[0]
    for j in range(piece_count):
        held = pieces[slot_ref[j]].astype(jnp.float32)
        rows[j * 3 * ROW_PITCH : (j + 1) * 3 * ROW_PITCH, :] = held[: 3 * ROW_PITCH]
    stack = 3 * piece_count
    scales = rows[pl.ds(lons, stack, stride=ROW_PITCH), :]

    def level_rows(lon):
        return rows[pl.ds(lon, stack, stride=ROW_PITCH), :] * scales[:, lon : lon + 1]

    met[last] = level_rows(last)
    east_c[...] = met[last, 0:levels, :]
    west_copy = pltpu.make_async_remote_copy(
        src_ref=east_c,
        dst_ref=west_c,
        send_sem=west_send,
        recv_sem=west_recv,
        device_id=east,
        device_id_type=MESH,
    )
    west_copy.start()
    for lon in range(last):
        met[lon] = level_rows(lon)

    lane = lax.broadcasted_iota(jnp.int32, (levels, lats), 1)
    level = lax.broadcasted_iota(jnp.int32, (levels, lats), 0)

    def east_parts(lon, before, here):
        la, lb, lc, ld = face_parts(before)
        ra, rb, rc, rd = face_parts(here)
        coef[lon, 0] = la
        coef[lon, 1] = lb - ra
        coef[lon, 2] = 1.0 + lc - rb
        coef[lon, 3] = ld - rc
        coef[lon, 4] = -rd

    def other_parts(lon):
        south = jnp.where(lane > 0, met[lon, levels : 2 * levels, :], 0.0)
        sa, sb, sc, sd = face_parts(south)
        ua, ub, uc, ud = (pltpu.roll(p, lats - 1, 1) for p in (sa, sb, sc, sd))
        air = 1.0 + 0.5 * met[lon, 2 * levels : 3 * levels, :]
        cloud = (level < top_ref[pl.ds(lon, 1), :]).astype(jnp.float32)
        strength = strength_ref[pl.ds(lon, 1), :]
        weighted = cloud * air
        mass = jnp.sum(weighted, axis=0, keepdims=True)
        keep = 1.0 - strength * cloud
        coef[lon, 5] = keep * jnp.where(lane > 1, sa, 0.0)
        coef[lon, 6] = keep * jnp.where(lane > 0, sb - ua, 0.0)
        coef[lon, 7] = keep * (1.0 + sc - ub)
        coef[lon, 8] = keep * jnp.where(lane < lats - 1, sd - uc, 0.0)
        coef[lon, 9] = keep * jnp.where(lane < lats - 2, -ud, 0.0)
        coef[lon, 10] = strength * weighted / (mass * keep)
        coef[lon, 11] = cloud

    group = 6

    def all_parts(n, _):
        for u in range(group):
            lon = n * group + u
            east_parts(lon, met[jnp.maximum(lon - 1, 0), 0:levels, :], met[lon, 0:levels, :])
            other_parts(lon)
        return 0

    lax.fori_loop(0, lons // group, all_parts, 0)

    shift = shift_ref[...]

    def inside(source, target, start, stop):
        def some(n, _):
            for u in range(PAIR):
                lon = start + n * PAIR + u
                parts = tuple(coef[lon, f] for f in range(FIELDS))
                around = [source[:, lon + d] for d in (-2, -1, 0, 1, 2)]
                target[:, lon] = column_step(around, parts, shift)
            return 0

        lax.fori_loop(0, (stop - start) // PAIR, some, 0)

    def edges(source, target, substep, blk):
        part = pl.ds(blk * block, block)

        def cell(place):
            if 0 <= place <= last:
                return source[part, place]
            way = EAST if place < 0 else WEST
            near = place in (-1, last + 1)
            if substep == 0:
                if near:
                    return near_in[way, part]
                return far_in[way, part].astype(jnp.float32)
            return halo_in[way, part, HIGH if near else LOW].astype(jnp.float32)

        for lon in (0, 1, last - 1, last):
            parts = [coef[lon, f] for f in range(FIELDS)]
            if substep == 1 and lon == 0:
                parts[0] = edge_coef[EAST]
            if substep == 1 and lon == last:
                parts[4] = edge_coef[WEST]
            around = [cell(lon + d) for d in (-2, -1, 0, 1, 2)]
            target[part, lon] = column_step(around, tuple(parts), shift)

    def halo_copy(way, blk):
        part = pl.ds(blk * block, block)
        return pltpu.make_async_remote_copy(
            src_ref=halo_out.at[way, part],
            dst_ref=halo_in.at[way, part],
            send_sem=halo_send.at[way, blk],
            recv_sem=halo_recv.at[way, blk],
            device_id=toward[way],
            device_id_type=MESH,
        )

    def stage(way, blk):
        part = pl.ds(blk * block, block)
        near, far = (last, last - 1) if way == EAST else (0, 1)
        bend = 0.25 * (1.0 - east_c[...]) if way == EAST else 0.25 * (1.0 + west_c[...])
        cell = q1[part, near]
        high = cell.astype(jnp.bfloat16)
        rest = (cell - high.astype(jnp.float32)) - bend * q1[part, far]
        halo_out[way, part, HIGH] = high
        halo_out[way, part, LOW] = rest.astype(jnp.bfloat16)

    middle = 2 + 6
    inside(q0, q1, 2, middle)

    west_copy.wait()
    east_parts(0, west_c[...], met[0, 0:levels, :])
    edge_coef[EAST] = jnp.maximum(west_c[...], 0.0)
    edge_coef[WEST] = -jnp.minimum(east_c[...], 0.0)

    def first_edges(blk):
        for way in (EAST, WEST):
            for copy in raw_copies(way, blk):
                copy.wait_recv()
        edges(q0, q1, 0, blk)
        for way in (EAST, WEST):
            stage(way, blk)
            halo_copy(way, blk).start()

    each_block(first_edges)
    inside(q0, q1, middle, lons - 2)
    inside(q1, out_ref, 2, lons - 2)

    def second_edges(blk):
        for way in (EAST, WEST):
            halo_copy(way, blk).wait_recv()
        edges(q1, out_ref, 1, blk)

    each_block(second_edges)

    def drain(blk):
        for way in (EAST, WEST):
            for copy in raw_copies(way, blk):
                copy.wait_send()
            halo_copy(way, blk).wait_send()

    each_block(drain)
    for copy in piece_copies:
        copy.wait_send()
    for k in range(chips):
        pass_on(k).wait_send()


def local(tracer_devices, space_devices, tracers, met_codes, met_scales, owner_slot, conv_weight,
          cloud_top, emission, region_tag):
    by_lon = jnp.transpose(tracers, (0, 2, 1, 3))
    count, lons, levels, lats = by_lon.shape
    pieces = owner_slot.shape[0]
    stack = pieces * met_codes.shape[1]
    chips = tracer_devices // CORES
    side = (2, count, levels, lats)
    halo = (2, count, 2, levels, lats)
    hbm = pl.BlockSpec(memory_space=pltpu.HBM)
    dma = pltpu.SemaphoreType.DMA
    out = pl.pallas_call(
        functools.partial(step_kernel, tracer_devices, space_devices),
        out_shape=jax.ShapeDtypeStruct(by_lon.shape, jnp.float32),
        in_specs=[hbm] * 8,
        out_specs=pl.BlockSpec(memory_space=pltpu.VMEM),
        scratch_shapes=[
            pltpu.VMEM(by_lon.shape, jnp.float32),
            pltpu.VMEM(by_lon.shape, jnp.float32),
            pltpu.VMEM(met_codes.shape, jnp.bfloat16),
            pltpu.VMEM(met_scales.shape, jnp.bfloat16),
            pltpu.SMEM(owner_slot.shape, jnp.int32),
            pltpu.VMEM(conv_weight.shape, jnp.float32),
            pltpu.VMEM(cloud_top.shape, jnp.int32),
            pltpu.VMEM(emission.shape, jnp.float32),
            pltpu.VMEM(region_tag.shape, jnp.int32),
            pltpu.VMEM((pieces, PIECE_ROWS, lats), jnp.bfloat16),
            pltpu.VMEM((PIECE_ROWS, lats), jnp.float32),
            pltpu.VMEM((pieces * 3 * ROW_PITCH, lats), jnp.float32),
            pltpu.VMEM((lons, stack, lats), jnp.float32),
            pltpu.VMEM((lons, FIELDS, levels, lats), jnp.float32),
            pltpu.VMEM((2, levels, lats), jnp.float32),
            pltpu.VMEM((2 * lats, 2 * lats), jnp.bfloat16),
            pltpu.VMEM((levels, lats), jnp.float32),
            pltpu.VMEM((levels, lats), jnp.float32),
            pltpu.VMEM(side, jnp.bfloat16),
            pltpu.VMEM(side, jnp.float32),
            pltpu.VMEM(side, jnp.bfloat16),
            pltpu.VMEM(halo, jnp.bfloat16),
            pltpu.VMEM(halo, jnp.bfloat16),
            dma((10,)),
            dma((chips,)),
            dma((chips,)),
            dma((chips,)),
            dma((chips,)),
            dma,
            dma,
            dma((2, 2, BLOCKS)),
            dma((2, 2, BLOCKS)),
            dma((2, BLOCKS)),
            dma((2, BLOCKS)),
        ],
        compiler_params=pltpu.CompilerParams(
            collective_id=0, has_side_effects=True, vmem_limit_bytes=48 * 1024 * 1024
        ),
        name="transport_step",
    )(
        *(
            pltpu.with_memory_space_constraint(x, pltpu.HBM)
            for x in (by_lon, met_codes, met_scales, owner_slot, conv_weight, cloud_top, emission)
            + (region_tag,)
        )
    )
    return jnp.transpose(out, (0, 2, 1, 3))


def solution(mesh):
    placed = (
        P("tracer", None, "space", None),
        P("tracer", None, "space", None),
        P("tracer", None, "space"),
        P(),
        P("space", None),
        P("space", None),
        P("space", None),
        P("space", None),
    )
    return jax.shard_map(
        functools.partial(local, mesh.shape["tracer"], mesh.shape["space"]),
        mesh=mesh,
        in_specs=placed,
        out_specs=P("tracer", None, "space", None),
        check_vma=False,
    )
```

time: 63.6 us -> 47.1 us (0.74)
  Pallas kernels: 56.1 us -> 44.8 us
  local copies, waits for them, and re-layouts: 7.07 us -> 2.19 us
    pallas_call x1, Pallas kernels: 56.1 us -> 44.8 us  [local(): pl.pallas_call(functools.partial(step_kernel, tracer_devices, space_devic...]
    unnamed x15 -> x1, local copies, waits for them, and re-layouts: 7.07 us -> 2.19 us
where the time goes in v2:
time: 47.1 us; the launch traced here: 47 us
  Pallas kernels  44.8 us (95%)
  local copies, waits for them, and re-layouts  2.19 us (5%)
    pallas_call x1, Pallas kernels, local(): pl.pallas_call(functools.partial(step_kernel, tracer_devices, space_devic...  44.8 us
    unnamed x1, local copies, waits for them, and re-layouts  2.19 us

profile of v2, /device:TPU:1, one launch (start us, length us, event | category | flops | bytes accessed | tf_op | source)
XLA Modules:
  0.0 47.0 jit_solution(11858364793459768689)
XLA Ops:
  0.0 44.8 %transport_step.1 = f32[32,18,16,128]{3,2,1,0:T(8,128)S(1)} custom-call(f32[32,18,16,128]{3,2,1,0:T(8,128)} %bitcast.3, bf16[1,3,18,128]{3,2,1,0:T(8,128)(2,1)} %codes_hbm.1, bf16[1,3,18]{2,1,0:T(4,128)(2,1)} %scales_hbm.1, s32[16]{0:T(128)} %slot_hbm.1, f32[18,128]{1,0:T(8,128)} %strength_hbm.1, s32[18,128]{1,0:T(8,128)} %top_hbm.1, ...), custom_call_target="tpu_custom_call" | custom-call | tf_op jit(solution)/shard_map/transport_step/pallas_call | solution.py:418
  44.8 2.2 %copy.10 = f32[32,16,18,128]{3,1,2,0:T(8,128)} copy(f32[32,16,18,128]{3,1,2,0:T(8,128)S(1)} %bitcast.2) | data formatting | bytes 9437184

commit v3 on v2

--- a/solution.py
+++ b/solution.py
@@ -10,7 +10,12 @@
 MESH = pl.DeviceIdType.MESH
 EAST, WEST = 0, 1
 HIGH, LOW = 0, 1
+NEAR, FAR = 0, 1
 BLOCKS = 4
+DIRECT = 5
+STEPS = 1200.0
+FLOOR = 24.0
+ROW = 4
 FIELDS = 12
 ROW_PITCH = 24
 PIECE_ROWS = 80
@@ -29,6 +34,19 @@
         jnp.where(up, bend, c),
         jnp.where(up, zero, bend),
     )
+
+
+def encoded(value):
+    size = jnp.maximum(jnp.abs(value), 2.0**-FLOOR)
+    steps = jnp.log2(size) * STEPS + (FLOOR * STEPS + 0.5)
+    steps = jnp.where(value < 0, -steps, steps)
+    return steps.astype(jnp.int32).astype(jnp.int16)
+
+
+def decoded(code):
+    steps = code.astype(jnp.int32).astype(jnp.float32)
+    size = jnp.exp2(jnp.abs(steps) * (1.0 / STEPS) - FLOOR)
+    return jnp.where(steps < 0, -size, size)
 
 
 def column_step(cells, parts, shift):
@@ -81,11 +99,12 @@
     shift_ref,
     west_c,
     east_c,
-    far_out,
-    near_in,
-    far_in,
+    raw_out,
+    raw_in,
+    raw_relay,
     halo_out,
     halo_in,
+    halo_relay,
     load_sem,
     piece_send,
     piece_recv,
@@ -93,10 +112,10 @@
     pass_recv,
     west_send,
     west_recv,
-    raw_send,
-    raw_recv,
-    halo_send,
-    halo_recv,
+    raw_sems,
+    raw_relay_sems,
+    halo_sems,
+    halo_relay_sems,
 ):
     count, lons, levels, lats = x_hbm.shape
     last = lons - 1
@@ -105,6 +124,16 @@
     east = {"space": lax.rem(s_me + 1, space_devices)}
     west = {"space": lax.rem(s_me + space_devices - 1, space_devices)}
     toward = (east, west)
+    place = lax.rem(s_me, ROW)
+    ends = (place == ROW - 1, place == 0)
+    edge = jnp.logical_or(ends[EAST], ends[WEST])
+
+    def along(step):
+        return {"space": lax.rem(s_me + step + space_devices, space_devices)}
+
+    hop = (along(1 - ROW), along(ROW - 1))
+    relay_way = jnp.where(ends[WEST], EAST, WEST)
+    onward = along(jnp.where(ends[WEST], ROW, -ROW))
     sibling = {"tracer": t_me + 1 - 2 * lax.rem(t_me, CORES)}
     chips = tracer_devices // CORES
     block = count // BLOCKS
@@ -137,6 +166,12 @@
     for to in (sibling, east, west):
         pl.semaphore_signal(barrier, inc=1, device_id=to, device_id_type=MESH)
 
+    @pl.when(edge)
+    def _():
+        other = along(jnp.where(ends[WEST], ROW - 1, 1 - ROW))
+        for to in (other, along(ROW), along(-ROW)):
+            pl.semaphore_signal(barrier, inc=1, device_id=to, device_id_type=MESH)
+
     staged[...] = jnp.zeros_like(staged)
     loads[0].wait()
     loads[1].wait()
@@ -147,7 +182,7 @@
         ].astype(jnp.float32)
     pieces[t_me] = staged[...].astype(jnp.bfloat16)
 
-    pl.semaphore_wait(barrier, chips - 1 + 3)
+    pl.semaphore_wait(barrier, chips - 1 + 3 + jnp.where(edge, 3, 0))
 
     def pass_on(k):
         held = pieces.at[peer(chips - k)]
@@ -191,47 +226,113 @@
 
         lax.fori_loop(0, BLOCKS, one, 0)
 
-    def raw_copies(way, blk):
-        part = pl.ds(blk * block, block)
-        near = q0.at[part, last if way == EAST else 0]
-        pairs = ((near, near_in.at[way, part]), (far_out.at[way, part], far_in.at[way, part]))
-        return [
-            pltpu.make_async_remote_copy(
-                src_ref=src,
-                dst_ref=dst,
-                send_sem=raw_send.at[n, way, blk],
-                recv_sem=raw_recv.at[n, way, blk],
+    def exchange(out, into, relay, sems, relay_sems):
+        def halves(blk):
+            start = blk * block
+            return pl.ds(start, DIRECT), pl.ds(start + DIRECT, block - DIRECT)
+
+        def straight(way, blk, n):
+            part = halves(blk)[n]
+            return pltpu.make_async_remote_copy(
+                src_ref=out.at[way, part],
+                dst_ref=into.at[way, part],
+                send_sem=sems.at[0, way, blk, n],
+                recv_sem=sems.at[1, way, blk, n],
                 device_id=toward[way],
                 device_id_type=MESH,
             )
-            for n, (src, dst) in enumerate(pairs)
-        ]
+
+        def detour(way, blk):
+            part = halves(blk)[1]
+            return pltpu.make_async_remote_copy(
+                src_ref=out.at[way, part],
+                dst_ref=relay.at[part],
+                send_sem=sems.at[0, way, blk, 1],
+                recv_sem=relay_sems.at[1, blk],
+                device_id=hop[way],
+                device_id_type=MESH,
+            )
+
+        def second_leg(blk):
+            part = halves(blk)[1]
+            return pltpu.make_async_remote_copy(
+                src_ref=relay.at[part],
+                dst_ref=into.at[relay_way, part],
+                send_sem=relay_sems.at[0, blk],
+                recv_sem=sems.at[1, relay_way, blk, 1],
+                device_id=onward,
+                device_id_type=MESH,
+            )
+
+        def start_relayed(blk):
+            for way in (EAST, WEST):
+
+                @pl.when(ends[way])
+                def _(way=way):
+                    detour(way, blk).start()
+
+                @pl.when(jnp.logical_not(ends[way]))
+                def _(way=way):
+                    straight(way, blk, 1).start()
+
+        def start_direct(blk):
+            for way in (EAST, WEST):
+                straight(way, blk, 0).start()
+
+        def forward(blk):
+            @pl.when(edge)
+            def _():
+                detour(EAST, blk).wait_recv()
+                second_leg(blk).start()
+
+        def receive(blk):
+            for way in (EAST, WEST):
+                for n in (0, 1):
+                    straight(way, blk, n).wait_recv()
+
+        def drain(blk):
+            for way in (EAST, WEST):
+                for n in (0, 1):
+                    straight(way, blk, n).wait_send()
+
+            @pl.when(edge)
+            def _():
+                second_leg(blk).wait_send()
+
+        return start_relayed, start_direct, forward, receive, drain
+
+    raw = exchange(raw_out, raw_in, raw_relay, raw_sems, raw_relay_sems)
+    halo = exchange(halo_out, halo_in, halo_relay, halo_sems, halo_relay_sems)
+    RELAYED, STRAIGHT, FORWARD, RECEIVE, DRAIN = range(5)
 
     cells[0].wait()
     cells[1].wait()
     for lon in (0, 1, last - 1, last):
         emit(lon)
-    far_out[EAST] = q0[:, last - 1].astype(jnp.bfloat16)
-    far_out[WEST] = q0[:, 1].astype(jnp.bfloat16)
-
     def first_sends(blk):
-        for way in (EAST, WEST):
-            for copy in raw_copies(way, blk):
-                copy.start()
+        part = pl.ds(blk * block, block)
+        for way, near, far in ((EAST, last, last - 1), (WEST, 0, 1)):
+            raw_out[way, part, NEAR] = encoded(q0[part, near])
+            raw_out[way, part, FAR] = encoded(q0[part, far])
+        raw[RELAYED](blk)
+        raw[STRAIGHT](blk)
 
     each_block(first_sends)
+
+    cells[2].wait()
+
+    def emit_inside(n, _):
+        emit(n + 2)
+        return 0
+
+    lax.fori_loop(0, lons - 4, emit_inside, 0)
+    raw[FORWARD](0)
 
     for k, copy in enumerate(piece_copies, 1):
         copy.wait_recv()
         pass_on(k).start()
-
-    cells[2].wait()
-
-    def emit_inside(n, _):
-        emit(n + 2)
-        return 0
-
-    lax.fori_loop(0, lons - 4, emit_inside, 0)
+    raw[FORWARD](1)
+    raw[FORWARD](2)
 
     source = lax.broadcasted_iota(jnp.int32, (2 * lats, 2 * lats), 0) % lats
     target = lax.broadcasted_iota(jnp.int32, (2 * lats, 2 * lats), 1)
@@ -262,6 +363,7 @@
         device_id_type=MESH,
     )
     west_copy.start()
+    raw[FORWARD](3)
     for lon in range(last):
         met[lon] = level_rows(lon)
 
@@ -327,11 +429,9 @@
                 return source[part, place]
             way = EAST if place < 0 else WEST
             near = place in (-1, last + 1)
-            if substep == 0:
-                if near:
-                    return near_in[way, part]
-                return far_in[way, part].astype(jnp.float32)
-            return halo_in[way, part, HIGH if near else LOW].astype(jnp.float32)
+            if substep == 1:
+                return halo_in[way, part, HIGH if near else LOW].astype(jnp.float32)
+            return decoded(raw_in[way, part, NEAR if near else FAR])
 
         for lon in (0, 1, last - 1, last):
             parts = [coef[lon, f] for f in range(FIELDS)]
@@ -341,17 +441,6 @@
                 parts[4] = edge_coef[WEST]
             around = [cell(lon + d) for d in (-2, -1, 0, 1, 2)]
             target[part, lon] = column_step(around, tuple(parts), shift)
-
-    def halo_copy(way, blk):
-        part = pl.ds(blk * block, block)
-        return pltpu.make_async_remote_copy(
-            src_ref=halo_out.at[way, part],
-            dst_ref=halo_in.at[way, part],
-            send_sem=halo_send.at[way, blk],
-            recv_sem=halo_recv.at[way, blk],
-            device_id=toward[way],
-            device_id_type=MESH,
-        )
 
     def stage(way, blk):
         part = pl.ds(blk * block, block)
@@ -363,41 +452,38 @@
         halo_out[way, part, HIGH] = high
         halo_out[way, part, LOW] = rest.astype(jnp.bfloat16)
 
-    middle = 2 + 6
-    inside(q0, q1, 2, middle)
-
     west_copy.wait()
     east_parts(0, west_c[...], met[0, 0:levels, :])
     edge_coef[EAST] = jnp.maximum(west_c[...], 0.0)
     edge_coef[WEST] = -jnp.minimum(east_c[...], 0.0)
 
     def first_edges(blk):
-        for way in (EAST, WEST):
-            for copy in raw_copies(way, blk):
-                copy.wait_recv()
+        raw[RECEIVE](blk)
         edges(q0, q1, 0, blk)
         for way in (EAST, WEST):
             stage(way, blk)
-            halo_copy(way, blk).start()
-
-    each_block(first_edges)
-    inside(q0, q1, middle, lons - 2)
-    inside(q1, out_ref, 2, lons - 2)
+        halo[RELAYED](blk)
+        halo[STRAIGHT](blk)
+
+    inside_stops = (2, 4, 8, 12, 16)
+    for blk in range(BLOCKS):
+        first_edges(blk)
+        if blk:
+            halo[FORWARD](blk - 1)
+        inside(q0, q1, inside_stops[blk], inside_stops[blk + 1])
+
+    halves = 2 + 4
+    inside(q1, out_ref, 2, halves)
+    halo[FORWARD](BLOCKS - 1)
+    inside(q1, out_ref, halves, lons - 2)
 
     def second_edges(blk):
-        for way in (EAST, WEST):
-            halo_copy(way, blk).wait_recv()
+        halo[RECEIVE](blk)
         edges(q1, out_ref, 1, blk)
 
     each_block(second_edges)
-
-    def drain(blk):
-        for way in (EAST, WEST):
-            for copy in raw_copies(way, blk):
-                copy.wait_send()
-            halo_copy(way, blk).wait_send()
-
-    each_block(drain)
+    each_block(raw[DRAIN])
+    each_block(halo[DRAIN])
     for copy in piece_copies:
         copy.wait_send()
     for k in range(chips):
@@ -411,8 +497,7 @@
     pieces = owner_slot.shape[0]
     stack = pieces * met_codes.shape[1]
     chips = tracer_devices // CORES
-    side = (2, count, levels, lats)
-    halo = (2, count, 2, levels, lats)
+    halo = (count, 2, levels, lats)
     hbm = pl.BlockSpec(memory_space=pltpu.HBM)
     dma = pltpu.SemaphoreType.DMA
     out = pl.pallas_call(
@@ -439,10 +524,11 @@
             pltpu.VMEM((2 * lats, 2 * lats), jnp.bfloat16),
             pltpu.VMEM((levels, lats), jnp.float32),
             pltpu.VMEM((levels, lats), jnp.float32),
-            pltpu.VMEM(side, jnp.bfloat16),
-            pltpu.VMEM(side, jnp.float32),
-            pltpu.VMEM(side, jnp.bfloat16),
-            pltpu.VMEM(halo, jnp.bfloat16),
+            pltpu.VMEM((2,) + halo, jnp.int16),
+            pltpu.VMEM((2,) + halo, jnp.int16),
+            pltpu.VMEM(halo, jnp.int16),
+            pltpu.VMEM((2,) + halo, jnp.bfloat16),
+            pltpu.VMEM((2,) + halo, jnp.bfloat16),
             pltpu.VMEM(halo, jnp.bfloat16),
             dma((10,)),
             dma((chips,)),
@@ -451,9 +537,9 @@
             dma((chips,)),
             dma,
             dma,
-            dma((2, 2, BLOCKS)),
-            dma((2, 2, BLOCKS)),
+            dma((2, 2, BLOCKS, 2)),
             dma((2, BLOCKS)),
+            dma((2, 2, BLOCKS, 2)),
             dma((2, BLOCKS)),
         ],
         compiler_params=pltpu.CompilerParams(

time: 47.1 us -> 40.8 us (0.87)
  the two profiles are of different devices: /device:TPU:1 before, /device:TPU:2 now
where the time goes in v3:
time: 40.8 us
  Pallas kernels  38.6 us (95%)
  local copies, waits for them, and re-layouts  2.19 us (5%)
    pallas_call x1, Pallas kernels, local(): pl.pallas_call(functools.partial(step_kernel, tracer_devices, space_devic...  38.6 us
    unnamed x1, local copies, waits for them, and re-layouts  2.19 us

profile of v3, /device:TPU:2, one launch (start us, length us, event | category | flops | bytes accessed | tf_op | source)
XLA Modules:
  0.0 40.8 jit_solution(6128516720313314188)
XLA Ops:
  0.0 38.6 %transport_step.1 = f32[32,18,16,128]{3,2,1,0:T(8,128)S(1)} custom-call(f32[32,18,16,128]{3,2,1,0:T(8,128)} %bitcast.3, bf16[1,3,18,128]{3,2,1,0:T(8,128)(2,1)} %codes_hbm.1, bf16[1,3,18]{2,1,0:T(4,128)(2,1)} %scales_hbm.1, s32[16]{0:T(128)} %slot_hbm.1, f32[18,128]{1,0:T(8,128)} %strength_hbm.1, s32[18,128]{1,0:T(8,128)} %top_hbm.1, ...), custom_call_target="tpu_custom_call" | custom-call | tf_op jit(solution)/shard_map/transport_step/pallas_call | solution.py:503
  38.6 2.2 %copy.10 = f32[32,16,18,128]{3,1,2,0:T(8,128)} copy(f32[32,16,18,128]{3,1,2,0:T(8,128)S(1)} %bitcast.2) | data formatting | bytes 9437184

commit v4 on v3

v4 whole, which is shorter than its diff:
```python
import functools

import jax
import jax.numpy as jnp
from jax import lax
from jax.experimental import pallas as pl
from jax.experimental.pallas import tpu as pltpu
from jax.sharding import PartitionSpec as P

MESH = pl.DeviceIdType.MESH
EAST, WEST = 0, 1
NEAR, FAR = 0, 1
RIM = 2
BLOCKS = 4
DIRECT = (5, 4)
STEPS = 1200.0
FLOOR = 24.0
ROW = 4
FIELDS = 12
ROW_GROUP = 16
CORES = 2
PAIR = 2


def face_parts(c):
    size = jnp.abs(c)
    bend = 0.25 * size * (1.0 - size)
    up = c > 0
    zero = jnp.zeros_like(c)
    return (
        jnp.where(up, -bend, zero),
        jnp.where(up, c, -bend),
        jnp.where(up, bend, c),
        jnp.where(up, zero, bend),
    )


def encoded(value):
    size = jnp.maximum(jnp.abs(value), 2.0**-FLOOR)
    steps = jnp.log2(size) * STEPS + (FLOOR * STEPS + 0.5)
    steps = jnp.where(value < 0, -steps, steps)
    return steps.astype(jnp.int32).astype(jnp.int16)


def decoded(code):
    steps = code.astype(jnp.int32).astype(jnp.float32)
    size = jnp.exp2(jnp.abs(steps) * (1.0 / STEPS) - FLOOR)
    return jnp.where(steps < 0, -size, size)


def column_step(cells, parts, shift):
    ea, eb, ec, ed, ee, na, nb, nc, nd, ne, share, cloud = parts
    x = ea * cells[0] + eb * cells[1] + ec * cells[2] + ed * cells[3] + ee * cells[4]
    count, levels, lats = x.shape
    high = x.astype(jnp.bfloat16)
    low = (x - high.astype(jnp.float32)).astype(jnp.bfloat16)
    both = jnp.concatenate([high, low], axis=-1).reshape(count * levels, 2 * lats)
    moved = jnp.dot(both, shift, preferred_element_type=jnp.float32)
    moved = moved.reshape(count, levels, 2 * lats)
    y = (
        nc * x
        + nb * pltpu.roll(x, 1, 2)
        + nd * pltpu.roll(x, lats - 1, 2)
        + na * moved[..., :lats]
        + ne * moved[..., lats:]
    )
    mean = jnp.sum(share * y, axis=-2, keepdims=True)
    return y + cloud * mean


def step_kernel(
    tracer_devices,
    space_devices,
    x_hbm,
    codes_hbm,
    scales_hbm,
    slot_hbm,
    strength_hbm,
    top_hbm,
    emission_hbm,
    tag_hbm,
    out_ref,
    q0,
    q1,
    codes_ref,
    scales_ref,
    slot_ref,
    strength_ref,
    top_ref,
    emission_ref,
    tag_ref,
    pieces,
    staged,
    rows,
    met,
    coef,
    shift_ref,
    sky_out,
    sky_in,
    wing_out,
    wing_in,
    wave_out,
    wave_in,
    wave_relay,
    load_sem,
    piece_send,
    piece_recv,
    pass_send,
    pass_recv,
    sky_sems,
    wing_sems,
    wave_sems,
    relay_sems,
):
    count, lons, levels, lats = x_hbm.shape
    last = lons - 1
    t_me = lax.axis_index("tracer")
    s_me = lax.axis_index("space")
    east = {"space": lax.rem(s_me + 1, space_devices)}
    west = {"space": lax.rem(s_me + space_devices - 1, space_devices)}
    toward = (east, west)
    place = lax.rem(s_me, ROW)
    ends = (place == ROW - 1, place == 0)
    edge = jnp.logical_or(ends[EAST], ends[WEST])

    def along(step):
        return {"space": lax.rem(s_me + step + space_devices, space_devices)}

    hop = (along(1 - ROW), along(ROW - 1))
    relay_way = jnp.where(ends[WEST], EAST, WEST)
    onward = along(jnp.where(ends[WEST], ROW, -ROW))
    sibling = {"tracer": t_me + 1 - 2 * lax.rem(t_me, CORES)}
    chips = tracer_devices // CORES
    block = count // BLOCKS
    level_rows = codes_hbm.shape[1]
    pitch = lons + 1
    piece_rows = level_rows * pitch

    def in_q0(lon):
        return lon + 2 * RIM

    def in_q1(lon):
        return lon + RIM

    def in_met(lon):
        return lon + RIM + 1

    def peer(k):
        return lax.rem(t_me + CORES * k, tracer_devices)

    small = (
        (codes_hbm, codes_ref),
        (scales_hbm, scales_ref),
        (tag_hbm, tag_ref),
        (emission_hbm, emission_ref),
        (slot_hbm, slot_ref),
        (strength_hbm, strength_ref),
        (top_hbm, top_ref),
    )
    loads = [
        pltpu.make_async_copy(src, dst, load_sem.at[n]) for n, (src, dst) in enumerate(small)
    ]
    rims = ((0, 2 * RIM), (lons - 2 * RIM, lons), (2 * RIM, lons - 2 * RIM))
    cells = [
        pltpu.make_async_copy(
            x_hbm.at[:, lo:hi], q0.at[:, in_q0(lo) : in_q0(hi)], load_sem.at[len(small) + n]
        )
        for n, (lo, hi) in enumerate(rims)
    ]
    for copy in loads + cells:
        copy.start()

    barrier = pltpu.get_barrier_semaphore()
    for k in range(1, chips):
        pl.semaphore_signal(barrier, inc=1, device_id={"tracer": peer(k)}, device_id_type=MESH)
    for to in (sibling, east, west):
        pl.semaphore_signal(barrier, inc=1, device_id=to, device_id_type=MESH)

    @pl.when(edge)
    def _():
        other = along(jnp.where(ends[WEST], ROW - 1, 1 - ROW))
        for to in (other, along(ROW), along(-ROW)):
            pl.semaphore_signal(barrier, inc=1, device_id=to, device_id_type=MESH)

    staged[...] = jnp.zeros_like(staged)
    loads[0].wait()
    loads[1].wait()
    for r in range(level_rows):
        at = r * pitch
        staged[at : at + lons, :] = codes_ref[0, r].astype(jnp.float32)
        staged[at + lons : at + lons + 1, 0:lons] = scales_ref[0, r : r + 1, :].astype(jnp.float32)
    pieces[t_me] = staged[...].astype(jnp.bfloat16)

    pl.semaphore_wait(barrier, chips - 1 + 3 + jnp.where(edge, 3, 0))

    def pass_on(k):
        held = pieces.at[peer(chips - k)]
        return pltpu.make_async_remote_copy(
            src_ref=held,
            dst_ref=held,
            send_sem=pass_send.at[k],
            recv_sem=pass_recv.at[k],
            device_id=sibling,
            device_id_type=MESH,
        )

    piece_copies = []
    for k in range(1, chips):
        copy = pltpu.make_async_remote_copy(
            src_ref=pieces.at[t_me],
            dst_ref=pieces.at[t_me],
            send_sem=piece_send.at[k],
            recv_sem=piece_recv.at[k],
            device_id={"tracer": peer(k)},
            device_id_type=MESH,
        )
        copy.start()
        piece_copies.append(copy)
    pass_on(0).start()

    for copy in loads[2:]:
        copy.wait()
    ids = t_me * count + lax.broadcasted_iota(jnp.int32, (count, 8, lats), 0)
    level_row = lax.broadcasted_iota(jnp.int32, (8, lats), 0)

    def emit(lon):
        tag = jnp.where(level_row == 0, tag_ref[pl.ds(lon, 1), :], -1)
        amount = jnp.broadcast_to(emission_ref[pl.ds(lon, 1), :], (8, lats))
        q0[:, in_q0(lon), 0:8, :] += jnp.where(tag[None] == ids, amount[None], 0.0)

    def each_block(act):
        def one(blk, _):
            act(blk)
            return 0

        lax.fori_loop(0, BLOCKS, one, 0)

    def wave(n):
        out, into, relay = wave_out.at[n], wave_in.at[n], wave_relay.at[n]

        def halves(blk):
            start = blk * block
            return pl.ds(start, DIRECT[n]), pl.ds(start + DIRECT[n], block - DIRECT[n])

        def straight(way, blk, h):
            part = halves(blk)[h]
            return pltpu.make_async_remote_copy(
                src_ref=out.at[way, part],
                dst_ref=into.at[way, part],
                send_sem=wave_sems.at[n, 0, way, blk, h],
                recv_sem=wave_sems.at[n, 1, way, blk, h],
                device_id=toward[way],
                device_id_type=MESH,
            )

        def detour(way, blk):
            part = halves(blk)[1]
            return pltpu.make_async_remote_copy(
                src_ref=out.at[way, part],
                dst_ref=relay.at[part],
                send_sem=wave_sems.at[n, 0, way, blk, 1],
                recv_sem=relay_sems.at[n, 1, blk],
                device_id=hop[way],
                device_id_type=MESH,
            )

        def second_leg(blk):
            part = halves(blk)[1]
            return pltpu.make_async_remote_copy(
                src_ref=relay.at[part],
                dst_ref=into.at[relay_way, part],
                send_sem=relay_sems.at[n, 0, blk],
                recv_sem=wave_sems.at[n, 1, relay_way, blk, 1],
                device_id=onward,
                device_id_type=MESH,
            )

        def send(blk):
            part = pl.ds(blk * block, block)
            for way in (EAST, WEST):
                for slot in (NEAR, FAR):
                    depth = 2 * n + slot
                    lon = last - depth if way == EAST else depth
                    out[way, part, slot] = encoded(q0[part, in_q0(lon)])
            for way in (EAST, WEST):

                @pl.when(ends[way])
                def _(way=way):
                    detour(way, blk).start()

                @pl.when(jnp.logical_not(ends[way]))
                def _(way=way):
                    straight(way, blk, 1).start()

            for way in (EAST, WEST):
                straight(way, blk, 0).start()

        def forward(blk):
            @pl.when(edge)
            def _():
                detour(EAST, blk).wait_recv()
                second_leg(blk).start()

        def receive(blk):
            part = pl.ds(blk * block, block)
            for way in (EAST, WEST):
                for h in (0, 1):
                    straight(way, blk, h).wait_recv()
                for slot in (NEAR, FAR):
                    depth = 2 * n + slot
                    lon = -1 - depth if way == EAST else lons + depth
                    q0[part, in_q0(lon)] = decoded(into[way, part, slot])

        def drain(blk):
            for way in (EAST, WEST):
                for h in (0, 1):
                    straight(way, blk, h).wait_send()

            @pl.when(edge)
            def _():
                second_leg(blk).wait_send()

        return send, forward, receive, drain

    waves = (wave(0), wave(1))
    SEND, FORWARD, RECEIVE, DRAIN = range(4)

    cells[0].wait()
    cells[1].wait()
    for lon in (0, 1, last - 1, last):
        emit(lon)
    each_block(waves[0][SEND])
    for lon in (2, 3, last - 3, last - 2):
        emit(lon)
    each_block(waves[1][SEND])

    def sky_copy(way):
        return pltpu.make_async_remote_copy(
            src_ref=sky_out.at[way],
            dst_ref=sky_in.at[way],
            send_sem=sky_sems.at[0, way],
            recv_sem=sky_sems.at[1, way],
            device_id=toward[way],
            device_id_type=MESH,
        )

    sky_out[...] = jnp.zeros_like(sky_out)
    for way in (EAST, WEST):
        for slot in (NEAR, FAR):
            lon = last - slot if way == EAST else slot
            sky_out[way, slot : slot + 1, :] = strength_ref[lon : lon + 1, :]
            sky_out[way, RIM + slot : RIM + slot + 1, :] = top_ref[lon : lon + 1, :].astype(
                jnp.float32
            )
        sky_copy(way).start()

    cells[2].wait()

    def emit_inside(n, _):
        emit(n + 2 * RIM)
        return 0

    lax.fori_loop(0, lons - 4 * RIM, emit_inside, 0)
    waves[0][FORWARD](0)

    for k, copy in enumerate(piece_copies, 1):
        copy.wait_recv()
        pass_on(k).start()
        if k == chips // 2:
            waves[0][FORWARD](1)
    waves[0][FORWARD](2)

    source = lax.broadcasted_iota(jnp.int32, (2 * lats, 2 * lats), 0) % lats
    target = lax.broadcasted_iota(jnp.int32, (2 * lats, 2 * lats), 1)
    wanted = jnp.where(target < lats, target - 2, target - lats + 2)
    shift_ref[...] = jnp.where(source == wanted, 1.0, 0.0).astype(jnp.bfloat16)

    waves[0][FORWARD](3)
    for k in range(chips):
        pass_on(k).wait_recv()

    piece_count = slot_ref.shape[0]
    for j in range(piece_count):
        held = pieces[slot_ref[j]].astype(jnp.float32)
        rows[j * piece_rows : (j + 1) * piece_rows, :] = held[:piece_rows]
    stack = level_rows * piece_count

    def code_column(lon):
        return rows[pl.ds(lon, stack, stride=pitch), :]

    scales = code_column(lons)

    def wing_copy(way):
        return pltpu.make_async_remote_copy(
            src_ref=wing_out.at[way],
            dst_ref=wing_in.at[way],
            send_sem=wing_sems.at[0, way],
            recv_sem=wing_sems.at[1, way],
            device_id=toward[way],
            device_id_type=MESH,
        )

    for way in (EAST, WEST):
        for slot in (NEAR, FAR):
            lon = last - slot if way == EAST else slot
            wing_out[way, slot * stack : (slot + 1) * stack] = code_column(lon).astype(jnp.bfloat16)
        wing_out[way, 2 * stack : 3 * stack] = scales.astype(jnp.bfloat16)
        third = code_column(last - 2)[0:levels, :]
        wing_out[way, 3 * stack :] = third.astype(jnp.bfloat16)
        wing_copy(way).start()

    for lon in range(lons):
        met[in_met(lon)] = code_column(lon) * scales[:, lon : lon + 1]

    lane = lax.broadcasted_iota(jnp.int32, (levels, lats), 1)
    level = lax.broadcasted_iota(jnp.int32, (levels, lats), 0)

    def east_parts(lon):
        at = in_q1(lon)
        la, lb, lc, ld = face_parts(met[in_met(lon - 1), 0:levels, :])
        ra, rb, rc, rd = face_parts(met[in_met(lon), 0:levels, :])
        coef[at, 0] = la
        coef[at, 1] = lb - ra
        coef[at, 2] = 1.0 + lc - rb
        coef[at, 3] = ld - rc
        coef[at, 4] = -rd

    def other_parts(lon, strength, top):
        at = in_q1(lon)
        column = met[in_met(lon)]
        south = jnp.where(lane > 0, column[levels : 2 * levels, :], 0.0)
        sa, sb, sc, sd = face_parts(south)
        ua, ub, uc, ud = (pltpu.roll(p, lats - 1, 1) for p in (sa, sb, sc, sd))
        air = 1.0 + 0.5 * column[2 * levels : 3 * levels, :]
        cloud = (level < top).astype(jnp.float32)
        weighted = cloud * air
        mass = jnp.sum(weighted, axis=0, keepdims=True)
        keep = 1.0 - strength * cloud
        coef[at, 5] = keep * jnp.where(lane > 1, sa, 0.0)
        coef[at, 6] = keep * jnp.where(lane > 0, sb - ua, 0.0)
        coef[at, 7] = keep * (1.0 + sc - ub)
        coef[at, 8] = keep * jnp.where(lane < lats - 1, sd - uc, 0.0)
        coef[at, 9] = keep * jnp.where(lane < lats - 2, -ud, 0.0)
        coef[at, 10] = strength * weighted / (mass * keep)
        coef[at, 11] = cloud

    def own_other_parts(lon):
        other_parts(lon, strength_ref[pl.ds(lon, 1), :], top_ref[pl.ds(lon, 1), :])

    def inside_parts(lon):
        east_parts(lon)
        own_other_parts(lon)

    group = (lons - 2) // 2

    def some_parts(n, _):
        for u in range(group):
            inside_parts(1 + n * group + u)
        return 0

    waves[1][FORWARD](0)
    lax.fori_loop(0, 2, some_parts, 0)
    inside_parts(last)
    own_other_parts(0)
    waves[1][FORWARD](1)

    def rim_parts(lon):
        way = EAST if lon < 0 else WEST
        slot = -1 - lon if lon < 0 else lon - lons
        east_parts(lon)
        other_parts(
            lon,
            sky_in[way, slot : slot + 1, :],
            sky_in[way, RIM + slot : RIM + slot + 1, :].astype(jnp.int32),
        )

    shift = shift_ref[...]

    def advance(substep, lon, part):
        parts = tuple(coef[in_q1(lon), f] for f in range(FIELDS))
        if substep == 0:
            around = [q0[part, in_q0(lon + d)] for d in (-2, -1, 0, 1, 2)]
            q1[part, in_q1(lon)] = column_step(around, parts, shift)
        else:
            around = [q1[part, in_q1(lon + d)] for d in (-2, -1, 0, 1, 2)]
            out_ref[part, lon] = column_step(around, parts, shift)

    def inside(substep, start, stop):
        def some(n, _):
            for u in range(PAIR):
                advance(substep, start + n * PAIR + u, slice(None))
            return 0

        lax.fori_loop(0, (stop - start) // PAIR, some, 0)

    border = (0, 1, last - 1, last)

    def first_border(blk):
        waves[0][RECEIVE](blk)
        for lon in border:
            advance(0, lon, pl.ds(blk * block, block))

    inside(0, 2, 6)
    waves[1][FORWARD](2)
    inside(0, 6, 10)
    waves[1][FORWARD](3)
    inside(0, 10, lons - 2)

    for way in (EAST, WEST):
        wing_copy(way).wait_recv()
        sky_copy(way).wait_recv()
        near_scales = wing_in[way, 2 * stack : 3 * stack].astype(jnp.float32)
        for slot in (NEAR, FAR):
            theirs = last - slot if way == EAST else slot
            lon = -1 - slot if way == EAST else lons + slot
            code = wing_in[way, slot * stack : (slot + 1) * stack].astype(jnp.float32)
            met[in_met(lon)] = code * near_scales[:, theirs : theirs + 1]
        if way == EAST:
            third = wing_in[way, 3 * stack :].astype(jnp.float32)
            met[0, 0:levels, :] = third * near_scales[0:levels, last - 2 : last - 1]
    east_parts(0)
    for lon in (-2, -1, lons, lons + 1):
        rim_parts(lon)

    each_block(first_border)
    inside(1, 2, lons - 2)

    def finish(blk):
        part = pl.ds(blk * block, block)
        waves[1][RECEIVE](blk)
        for lon in (-2, -1, lons, lons + 1):
            advance(0, lon, part)
        for lon in border:
            advance(1, lon, part)

    each_block(finish)
    each_block(waves[0][DRAIN])
    each_block(waves[1][DRAIN])
    for way in (EAST, WEST):
        sky_copy(way).wait_send()
        wing_copy(way).wait_send()
    for copy in piece_copies:
        copy.wait_send()
    for k in range(chips):
        pass_on(k).wait_send()


def local(tracer_devices, space_devices, tracers, met_codes, met_scales, owner_slot, conv_weight,
          cloud_top, emission, region_tag):
    by_lon = jnp.transpose(tracers, (0, 2, 1, 3))
    count, lons, levels, lats = by_lon.shape
    pieces = owner_slot.shape[0]
    stack = pieces * met_codes.shape[1]
    chips = tracer_devices // CORES
    halo = (count, 2, levels, lats)
    wing = 3 * stack + levels
    piece_rows = met_codes.shape[1] * (lons + 1)
    sent_rows = pl.cdiv(piece_rows, ROW_GROUP) * ROW_GROUP
    hbm = pl.BlockSpec(memory_space=pltpu.HBM)
    dma = pltpu.SemaphoreType.DMA
    out = pl.pallas_call(
        functools.partial(step_kernel, tracer_devices, space_devices),
        out_shape=jax.ShapeDtypeStruct(by_lon.shape, jnp.float32),
        in_specs=[hbm] * 8,
        out_specs=pl.BlockSpec(memory_space=pltpu.VMEM),
        scratch_shapes=[
            pltpu.VMEM((count, lons + 4 * RIM, levels, lats), jnp.float32),
            pltpu.VMEM((count, lons + 2 * RIM, levels, lats), jnp.float32),
            pltpu.VMEM(met_codes.shape, jnp.bfloat16),
            pltpu.VMEM(met_scales.shape, jnp.bfloat16),
            pltpu.SMEM(owner_slot.shape, jnp.int32),
            pltpu.VMEM(conv_weight.shape, jnp.float32),
            pltpu.VMEM(cloud_top.shape, jnp.int32),
            pltpu.VMEM(emission.shape, jnp.float32),
            pltpu.VMEM(region_tag.shape, jnp.int32),
            pltpu.VMEM((pieces, sent_rows, lats), jnp.bfloat16),
            pltpu.VMEM((sent_rows, lats), jnp.float32),
            pltpu.VMEM((pieces * piece_rows, lats), jnp.float32),
            pltpu.VMEM((lons + 2 * RIM + 1, stack, lats), jnp.float32),
            pltpu.VMEM((lons + 2 * RIM, FIELDS, levels, lats), jnp.float32),
            pltpu.VMEM((2 * lats, 2 * lats), jnp.bfloat16),
            pltpu.VMEM((2, 8, lats), jnp.float32),
            pltpu.VMEM((2, 8, lats), jnp.float32),
            pltpu.VMEM((2, wing, lats), jnp.bfloat16),
            pltpu.VMEM((2, wing, lats), jnp.bfloat16),
            pltpu.VMEM((2, 2) + halo, jnp.int16),
            pltpu.VMEM((2, 2) + halo, jnp.int16),
            pltpu.VMEM((2,) + halo, jnp.int16),
            dma((10,)),
            dma((chips,)),
            dma((chips,)),
            dma((chips,)),
            dma((chips,)),
            dma((2, 2)),
            dma((2, 2)),
            dma((2, 2, 2, BLOCKS, 2)),
            dma((2, 2, BLOCKS)),
        ],
        compiler_params=pltpu.CompilerParams(
            collective_id=0, has_side_effects=True, vmem_limit_bytes=48 * 1024 * 1024
        ),
        name="transport_step",
    )(
        *(
            pltpu.with_memory_space_constraint(x, pltpu.HBM)
            for x in (by_lon, met_codes, met_scales, owner_slot, conv_weight, cloud_top, emission)
            + (region_tag,)
        )
    )
    return jnp.transpose(out, (0, 2, 1, 3))


def solution(mesh):
    placed = (
        P("tracer", None, "space", None),
        P("tracer", None, "space", None),
        P("tracer", None, "space"),
        P(),
        P("space", None),
        P("space", None),
        P("space", None),
        P("space", None),
    )
    return jax.shard_map(
        functools.partial(local, mesh.shape["tracer"], mesh.shape["space"]),
        mesh=mesh,
        in_specs=placed,
        out_specs=P("tracer", None, "space", None),
        check_vma=False,
    )
```

time: 40.8 us -> 40 us (0.980)
  the two profiles are of different devices: /device:TPU:2 before, /device:TPU:1 now
where the time goes in v4:
time: 40 us; the launch traced here: 39.7 us
  Pallas kernels  37.5 us (94%)
  local copies, waits for them, and re-layouts  2.19 us (5%)
    pallas_call x1, Pallas kernels, local(): pl.pallas_call(functools.partial(step_kernel, tracer_devices, space_devic...  37.5 us
    unnamed x1, local copies, waits for them, and re-layouts  2.19 us

profile of v4, /device:TPU:1, one launch (start us, length us, event | category | flops | bytes accessed | tf_op | source)
XLA Modules:
  0.0 39.7 jit_solution(14912358881721592659)
XLA Ops:
  0.0 37.5 %transport_step.1 = f32[32,18,16,128]{3,2,1,0:T(8,128)S(1)} custom-call(f32[32,18,16,128]{3,2,1,0:T(8,128)} %bitcast.3, bf16[1,3,18,128]{3,2,1,0:T(8,128)(2,1)} %codes_hbm.1, bf16[1,3,18]{2,1,0:T(4,128)(2,1)} %scales_hbm.1, s32[16]{0:T(128)} %slot_hbm.1, f32[18,128]{1,0:T(8,128)} %strength_hbm.1, s32[18,128]{1,0:T(8,128)} %top_hbm.1, ...), custom_call_target="tpu_custom_call" | custom-call | tf_op jit(solution)/shard_map/transport_step/pallas_call | solution.py:561
  37.5 2.2 %copy.10 = f32[32,16,18,128]{3,1,2,0:T(8,128)} copy(f32[32,16,18,128]{3,1,2,0:T(8,128)S(1)} %bitcast.2) | data formatting | bytes 9437184

commit v5 on v4

--- a/solution.py
+++ b/solution.py
@@ -12,7 +12,7 @@
 NEAR, FAR = 0, 1
 RIM = 2
 BLOCKS = 4
-DIRECT = (5, 4)
+DIRECT = (3, 2)
 STEPS = 1200.0
 FLOOR = 24.0
 ROW = 4
@@ -167,7 +167,7 @@
         )
         for n, (lo, hi) in enumerate(rims)
     ]
-    for copy in loads + cells:
+    for copy in loads + cells[:2]:
         copy.start()
 
     barrier = pltpu.get_barrier_semaphore()
@@ -301,15 +301,22 @@
                 detour(EAST, blk).wait_recv()
                 second_leg(blk).start()
 
-        def receive(blk):
+        def receive(way, blk):
             part = pl.ds(blk * block, block)
-            for way in (EAST, WEST):
-                for h in (0, 1):
-                    straight(way, blk, h).wait_recv()
-                for slot in (NEAR, FAR):
-                    depth = 2 * n + slot
-                    lon = -1 - depth if way == EAST else lons + depth
-                    q0[part, in_q0(lon)] = decoded(into[way, part, slot])
+            for h in (0, 1):
+                piece = halves(blk)[h]
+                pltpu.make_async_remote_copy(
+                    src_ref=out.at[way, piece],
+                    dst_ref=into.at[way, piece],
+                    send_sem=wave_sems.at[n, 0, way, blk, h],
+                    recv_sem=wave_sems.at[n, 1, way, blk, h],
+                    device_id=east,
+                    device_id_type=MESH,
+                ).wait_recv()
+            for slot in (NEAR, FAR):
+                depth = 2 * n + slot
+                lon = jnp.where(way == EAST, -1 - depth, lons + depth)
+                q0[part, in_q0(lon)] = decoded(into[way, part, slot])
 
         def drain(blk):
             for way in (EAST, WEST):
@@ -327,12 +334,22 @@
 
     cells[0].wait()
     cells[1].wait()
+    cells[2].start()
     for lon in (0, 1, last - 1, last):
         emit(lon)
     each_block(waves[0][SEND])
+    def take_pieces(start, stop):
+        for k in range(start, stop):
+            piece_copies[k - 1].wait_recv()
+            pass_on(k).start()
+
     for lon in (2, 3, last - 3, last - 2):
         emit(lon)
     each_block(waves[1][SEND])
+    waves[0][FORWARD](0)
+    take_pieces(1, chips // 2)
+    waves[0][FORWARD](1)
+    take_pieces(chips // 2, chips)
 
     def sky_copy(way):
         return pltpu.make_async_remote_copy(
@@ -361,13 +378,6 @@
         return 0
 
     lax.fori_loop(0, lons - 4 * RIM, emit_inside, 0)
-    waves[0][FORWARD](0)
-
-    for k, copy in enumerate(piece_copies, 1):
-        copy.wait_recv()
-        pass_on(k).start()
-        if k == chips // 2:
-            waves[0][FORWARD](1)
     waves[0][FORWARD](2)
 
     source = lax.broadcasted_iota(jnp.int32, (2 * lats, 2 * lats), 0) % lats
@@ -459,10 +469,12 @@
         return 0
 
     waves[1][FORWARD](0)
+    waves[1][FORWARD](1)
     lax.fori_loop(0, 2, some_parts, 0)
     inside_parts(last)
     own_other_parts(0)
-    waves[1][FORWARD](1)
+    waves[1][FORWARD](2)
+    waves[1][FORWARD](3)
 
     def rim_parts(lon):
         way = EAST if lon < 0 else WEST
@@ -496,15 +508,12 @@
     border = (0, 1, last - 1, last)
 
     def first_border(blk):
-        waves[0][RECEIVE](blk)
+        for way in (EAST, WEST):
+            waves[0][RECEIVE](way, blk)
         for lon in border:
             advance(0, lon, pl.ds(blk * block, block))
 
-    inside(0, 2, 6)
-    waves[1][FORWARD](2)
-    inside(0, 6, 10)
-    waves[1][FORWARD](3)
-    inside(0, 10, lons - 2)
+    inside(0, 2, lons - 2)
 
     for way in (EAST, WEST):
         wing_copy(way).wait_recv()
@@ -525,15 +534,19 @@
     each_block(first_border)
     inside(1, 2, lons - 2)
 
-    def finish(blk):
-        part = pl.ds(blk * block, block)
-        waves[1][RECEIVE](blk)
-        for lon in (-2, -1, lons, lons + 1):
-            advance(0, lon, part)
-        for lon in border:
-            advance(1, lon, part)
-
-    each_block(finish)
+    def finish(way, start, stop):
+        part = pl.ds(start * block, (stop - start) * block)
+        for blk in range(start, stop):
+            waves[1][RECEIVE](way, blk)
+        for depth in (0, 1):
+            advance(0, jnp.where(way == EAST, -1 - depth, lons + depth), part)
+        for depth in (0, 1):
+            advance(1, jnp.where(way == EAST, depth, last - depth), part)
+
+    late = jnp.where(ends[WEST], EAST, WEST)
+    finish(1 - late, 0, BLOCKS)
+    finish(late, 0, BLOCKS // 2)
+    finish(late, BLOCKS // 2, BLOCKS)
     each_block(waves[0][DRAIN])
     each_block(waves[1][DRAIN])
     for way in (EAST, WEST):

time: 40 us -> 37 us (0.925)
  the two profiles are of different devices: /device:TPU:1 before, /device:TPU:36 now
where the time goes in v5:
time: 37 us; the launch traced here: 36.9 us
  Pallas kernels  34.7 us (94%)
  local copies, waits for them, and re-layouts  2.19 us (6%)
    pallas_call x1, Pallas kernels, local(): pl.pallas_call(functools.partial(step_kernel, tracer_devices, space_devic...  34.7 us
    unnamed x1, local copies, waits for them, and re-layouts  2.19 us

profile of v5, /device:TPU:36, one launch (start us, length us, event | category | flops | bytes accessed | tf_op | source)
XLA Modules:
  0.0 36.9 jit_solution(16188825668962046136)
XLA Ops:
  0.0 34.7 %transport_step.1 = f32[32,18,16,128]{3,2,1,0:T(8,128)S(1)} custom-call(f32[32,18,16,128]{3,2,1,0:T(8,128)} %bitcast.3, bf16[1,3,18,128]{3,2,1,0:T(8,128)(2,1)} %codes_hbm.1, bf16[1,3,18]{2,1,0:T(4,128)(2,1)} %scales_hbm.1, s32[16]{0:T(128)} %slot_hbm.1, f32[18,128]{1,0:T(8,128)} %strength_hbm.1, s32[18,128]{1,0:T(8,128)} %top_hbm.1, ...), custom_call_target="tpu_custom_call" | custom-call | tf_op jit(solution)/shard_map/transport_step/pallas_call | solution.py:574
  34.8 2.2 %copy.10 = f32[32,16,18,128]{3,1,2,0:T(8,128)} copy(f32[32,16,18,128]{3,1,2,0:T(8,128)S(1)} %bitcast.2) | data formatting | bytes 9437184

commit v6 on v5

--- a/solution.py
+++ b/solution.py
@@ -12,7 +12,7 @@
 NEAR, FAR = 0, 1
 RIM = 2
 BLOCKS = 4
-DIRECT = (3, 2)
+DIRECT = (4, 2)
 STEPS = 1200.0
 FLOOR = 24.0
 ROW = 4
@@ -160,14 +160,15 @@
     loads = [
         pltpu.make_async_copy(src, dst, load_sem.at[n]) for n, (src, dst) in enumerate(small)
     ]
-    rims = ((0, 2 * RIM), (lons - 2 * RIM, lons), (2 * RIM, lons - 2 * RIM))
+    cuts = (0, RIM, 2 * RIM, lons - 2 * RIM, lons - RIM, lons)
+    rims = [cuts[n : n + 2] for n in (0, 4, 1, 3, 2)]
     cells = [
         pltpu.make_async_copy(
             x_hbm.at[:, lo:hi], q0.at[:, in_q0(lo) : in_q0(hi)], load_sem.at[len(small) + n]
         )
         for n, (lo, hi) in enumerate(rims)
     ]
-    for copy in loads + cells[:2]:
+    for copy in loads + cells[:4]:
         copy.start()
 
     barrier = pltpu.get_barrier_semaphore()
@@ -334,7 +335,7 @@
 
     cells[0].wait()
     cells[1].wait()
-    cells[2].start()
+    cells[4].start()
     for lon in (0, 1, last - 1, last):
         emit(lon)
     each_block(waves[0][SEND])
@@ -343,6 +344,8 @@
             piece_copies[k - 1].wait_recv()
             pass_on(k).start()
 
+    cells[2].wait()
+    cells[3].wait()
     for lon in (2, 3, last - 3, last - 2):
         emit(lon)
     each_block(waves[1][SEND])
@@ -371,7 +374,7 @@
             )
         sky_copy(way).start()
 
-    cells[2].wait()
+    cells[4].wait()
 
     def emit_inside(n, _):
         emit(n + 2 * RIM)
@@ -401,9 +404,10 @@
     scales = code_column(lons)
 
     def wing_copy(way):
+        part = pl.ds(0, 3 * stack + (levels if way == EAST else 0))
         return pltpu.make_async_remote_copy(
-            src_ref=wing_out.at[way],
-            dst_ref=wing_in.at[way],
+            src_ref=wing_out.at[way, part],
+            dst_ref=wing_in.at[way, part],
             send_sem=wing_sems.at[0, way],
             recv_sem=wing_sems.at[1, way],
             device_id=toward[way],
@@ -415,8 +419,9 @@
             lon = last - slot if way == EAST else slot
             wing_out[way, slot * stack : (slot + 1) * stack] = code_column(lon).astype(jnp.bfloat16)
         wing_out[way, 2 * stack : 3 * stack] = scales.astype(jnp.bfloat16)
-        third = code_column(last - 2)[0:levels, :]
-        wing_out[way, 3 * stack :] = third.astype(jnp.bfloat16)
+        if way == EAST:
+            third = code_column(last - 2)[0:levels, :]
+            wing_out[way, 3 * stack :] = third.astype(jnp.bfloat16)
         wing_copy(way).start()
 
     for lon in range(lons):
@@ -425,15 +430,19 @@
     lane = lax.broadcasted_iota(jnp.int32, (levels, lats), 1)
     level = lax.broadcasted_iota(jnp.int32, (levels, lats), 0)
 
-    def east_parts(lon):
+    def face(lon):
+        return face_parts(met[in_met(lon), 0:levels, :])
+
+    def east_parts(lon, left=None):
         at = in_q1(lon)
-        la, lb, lc, ld = face_parts(met[in_met(lon - 1), 0:levels, :])
-        ra, rb, rc, rd = face_parts(met[in_met(lon), 0:levels, :])
+        la, lb, lc, ld = face(lon - 1) if left is None else left
+        ra, rb, rc, rd = right = face(lon)
         coef[at, 0] = la
         coef[at, 1] = lb - ra
         coef[at, 2] = 1.0 + lc - rb
         coef[at, 3] = ld - rc
         coef[at, 4] = -rd
+        return right
 
     def other_parts(lon, strength, top):
         at = in_q1(lon)
@@ -457,15 +466,17 @@
     def own_other_parts(lon):
         other_parts(lon, strength_ref[pl.ds(lon, 1), :], top_ref[pl.ds(lon, 1), :])
 
-    def inside_parts(lon):
-        east_parts(lon)
+    def inside_parts(lon, left=None):
+        right = east_parts(lon, left)
         own_other_parts(lon)
+        return right
 
     group = (lons - 2) // 2
 
     def some_parts(n, _):
+        left = None
         for u in range(group):
-            inside_parts(1 + n * group + u)
+            left = inside_parts(1 + n * group + u, left)
         return 0
 
     waves[1][FORWARD](0)
@@ -507,11 +518,12 @@
 
     border = (0, 1, last - 1, last)
 
-    def first_border(blk):
+    def first_border(half):
         for way in (EAST, WEST):
-            waves[0][RECEIVE](way, blk)
+            for u in (0, 1):
+                waves[0][RECEIVE](way, 2 * half + u)
         for lon in border:
-            advance(0, lon, pl.ds(blk * block, block))
+            advance(0, lon, pl.ds(half * 2 * block, 2 * block))
 
     inside(0, 2, lons - 2)
 
@@ -531,7 +543,8 @@
     for lon in (-2, -1, lons, lons + 1):
         rim_parts(lon)
 
-    each_block(first_border)
+    for half in range(BLOCKS // 2):
+        first_border(half)
     inside(1, 2, lons - 2)
 
     def finish(way, start, stop):
@@ -599,7 +612,7 @@
             pltpu.VMEM((2, 2) + halo, jnp.int16),
             pltpu.VMEM((2, 2) + halo, jnp.int16),
             pltpu.VMEM((2,) + halo, jnp.int16),
-            dma((10,)),
+            dma((12,)),
             dma((chips,)),
             dma((chips,)),
             dma((chips,)),

time: 37 us -> 37 us (level)
  the two profiles are of different devices: /device:TPU:36 before, /device:TPU:6 now
where the time goes in v6:
time: 37 us; the launch traced here: 36.9 us
  Pallas kernels  34.7 us (94%)
  local copies, waits for them, and re-layouts  2.19 us (6%)
    pallas_call x1, Pallas kernels, local(): pl.pallas_call(functools.partial(step_kernel, tracer_devices, space_devic...  34.7 us
    unnamed x1, local copies, waits for them, and re-layouts  2.19 us

profile of v6, /device:TPU:6, one launch (start us, length us, event | category | flops | bytes accessed | tf_op | source)
XLA Modules:
  0.0 36.9 jit_solution(11697203708842426328)
XLA Ops:
  0.0 34.7 %transport_step.1 = f32[32,18,16,128]{3,2,1,0:T(8,128)S(1)} custom-call(f32[32,18,16,128]{3,2,1,0:T(8,128)} %bitcast.3, bf16[1,3,18,128]{3,2,1,0:T(8,128)(2,1)} %codes_hbm.1, bf16[1,3,18]{2,1,0:T(4,128)(2,1)} %scales_hbm.1, s32[16]{0:T(128)} %slot_hbm.1, f32[18,128]{1,0:T(8,128)} %strength_hbm.1, s32[18,128]{1,0:T(8,128)} %top_hbm.1, ...), custom_call_target="tpu_custom_call" | custom-call | tf_op jit(solution)/shard_map/transport_step/pallas_call | solution.py:587
  34.7 2.2 %copy.10 = f32[32,16,18,128]{3,1,2,0:T(8,128)} copy(f32[32,16,18,128]{3,1,2,0:T(8,128)S(1)} %bitcast.2) | data formatting | bytes 9437184
